TPU v7x, 128 devices: a whole 4x4x4 slice. The times are simulated.
128 devices in a mesh: tm: 2 (over x_lo), space: 64 (over y, z, x_hi, core).
Axes of the slice: x: 4 (x_hi: 2, x_lo: 2; x = x_hi * 2 + x_lo), y: 4, z: 4, core: 2. Of those that a mesh axis runs over, the one named last changes fastest.
Arguments:
- initial: float32 [2, 128, 128, 128], P(None, 'space'), may hold values from 0 to 1
- kappa: float32 [128, 128, 128], P('space'), may hold values from 0.1 to 1
Outputs:
- ends: float32 [2, 2, 128, 128, 128], P('tm', None, 'space')
All inputs are finite; a program needn't handle non-finite values.
Results may differ from a plain program's by a relative error of at most 0.0001.
Values sent between devices are 32-bit elements; how exact they have to be, the bound alone decides.
A program may use at most 128 MiB of HBM per device.

v0:
```python
import jax
import jax.numpy as jnp
from jax import lax
from jax.sharding import PartitionSpec as P

ITERS = 2


STEP = 0.25
HALF = 0.125
FEED = 0.04
KILL = 0.06
WEIGHTS = ((5.0 / 24.0, 1.0 / 3.0, -1.0 / 24.0), (-1.0 / 24.0, 1.0 / 3.0, 5.0 / 24.0))


def padded_2(block, sides, width):
    for axis, dim in sides:
        count = lax.axis_size(axis)
        forward = [(i, i + 1) for i in range(count - 1)]
        backward = [(target, source) for source, target in forward]
        low = lax.ppermute(
            lax.slice_in_dim(block, block.shape[dim] - width, None, axis=dim), axis, forward
        )
        high = lax.ppermute(lax.slice_in_dim(block, 0, width, axis=dim), axis, backward)
        block = jnp.concatenate([low, block, high], axis=dim)
    return block


def passed_along(value, axis, steps):
    count = lax.axis_size(axis)
    first, last = (max(0, -steps), min(count, count - steps))
    return lax.ppermute(value, axis, [(source, source + steps) for source in range(first, last)])


def react(padded, kappa, spacing):
    widths = [(0, 0)] * (padded.ndim - 2) + [(1, 1), (1, 1)]
    full = jnp.pad(padded, widths)
    centre = full[..., 1:-1, 1:-1, 1:-1]
    near = full[..., 2:, 1:-1, 1:-1] + full[..., :-2, 1:-1, 1:-1]
    near = near + full[..., 1:-1, 2:, 1:-1] + full[..., 1:-1, :-2, 1:-1]
    near = near + full[..., 1:-1, 1:-1, 2:] + full[..., 1:-1, 1:-1, :-2]
    laplace = (near - 6.0 * centre) / (spacing * spacing)
    first = centre[..., 0, :, :, :]
    second = centre[..., 1, :, :, :]
    source = first * second * second
    rate_a = kappa * laplace[..., 0, :, :, :] - source + FEED * (1.0 - first)
    rate_b = 0.5 * kappa * laplace[..., 1, :, :, :] + source - (FEED + KILL) * second
    return jnp.stack([rate_a, rate_b], axis=-4)


def restrict(field):
    shape = field.shape
    lead = shape[:-3]
    blocks = field.reshape(lead + (shape[-3] // 2, 2, shape[-2] // 2, 2, shape[-1] // 2, 2))
    return 0.125 * jnp.sum(blocks, axis=(-5, -3, -1))


def prolong(field):
    return jnp.repeat(jnp.repeat(jnp.repeat(field, 2, axis=-3), 2, axis=-2), 2, axis=-1)


def integrate(rates, row):
    return STEP * (
        WEIGHTS[row][0] * rates[0] + WEIGHTS[row][1] * rates[1] + WEIGHTS[row][2] * rates[2]
    )


def fine_rate(state, kappa):
    padded = padded_2(state, (("space", 1),), 1)
    return react(padded, kappa, 1.0)


def node_rates(nodes, kappa):
    stacked = jnp.stack(nodes)
    padded = padded_2(stacked, (("space", 2),), 1)
    rates = react(padded, kappa, 1.0)
    return [rates[0], rates[1], rates[2]]


def coarse_rate(state, coarse_kappa):
    padded = padded_2(state, (("space", 1),), 1)
    return react(padded, coarse_kappa, 2.0)


def coarse_node_rates(states, coarse_kappa):
    stacked = jnp.stack(states)
    padded = padded_2(stacked, (("space", 2),), 1)
    rates = react(padded, coarse_kappa, 2.0)
    return [rates[0], rates[1]]


def shards(initial, kappa):
    leading = lax.axis_index("tm") == 0
    slices = lax.axis_size("tm")
    coarse_kappa = restrict(kappa)
    coarse_initial = restrict(initial)
    nodes = [initial, initial, initial]
    start = initial
    for step in range(ITERS):
        if step > 0:
            arrived = passed_along(nodes[2], "tm", 1)
            start = jnp.where(leading, initial, arrived)
            old = node_rates(nodes, kappa)
            opening = fine_rate(start, kappa)
        else:
            opening = fine_rate(initial, kappa)
            old = [opening, opening, opening]
        values = [start]
        rates = [opening]
        for row in range(2):
            values.append(values[row] + HALF * (rates[row] - old[row]) + integrate(old, row))
            rates.append(fine_rate(values[row + 1], kappa))
        coarse_w = [restrict(value) for value in values]
        folded = [restrict(integrate(rates, row)) for row in range(2)]
        rate_w = coarse_node_rates(coarse_w[:2], coarse_kappa)
        received = jnp.zeros_like(coarse_initial)
        coarse = []
        for section in range(slices):
            coarse = [jnp.where(leading, coarse_initial, received)]
            for row in range(2):
                coarse.append(
                    coarse[row]
                    + HALF * (coarse_rate(coarse[row], coarse_kappa) - rate_w[row])
                    + folded[row]
                )
            if section + 1 < slices:
                received = passed_along(coarse[2], "tm", 1)
        nodes = [values[row] + prolong(coarse[row] - coarse_w[row]) for row in range(3)]
    return nodes[2][None]


def solution(mesh):
    return jax.shard_map(
        shards,
        mesh=mesh,
        in_specs=(P(None, "space", None, None), P("space", None, None)),
        out_specs=P("tm", None, "space", None, None),
        check_vma=False,
    )
```

profile of v0, /device:TPU:27, one launch (start us, length us, event | category | flops | bytes accessed | tf_op | source)
XLA Modules:
  0.0 504.1 jit_solution(13319297508429959320)
XLA Ops:
  13.9 9.8 %stack.163 = f32[1,1,2,64,2,64,2]{6,5,4,3,2,1,0:T(8,128)} reshape(f32[2,128,128]{2,1,0:T(8,128)S(1)} %get-tuple-element.38) | data formatting | bytes 262144 | tf_op jit(solution)/shard_map/stack | solution.py:48
  23.6 9.7 %stack.162 = f32[1,1,2,64,2,64,2]{6,5,4,3,2,1,0:T(8,128)} reshape(f32[2,128,128]{2,1,0:T(8,128)S(1)} %get-tuple-element.37) | data formatting | bytes 262144 | tf_op jit(solution)/shard_map/stack | solution.py:48
  33.4 9.8 %reduce_sum.125 = f32[2,64,2,64,2]{4,3,2,1,0:T(8,128)} reshape(f32[2,128,128]{2,1,0:T(8,128)S(1)} %get-tuple-element.50) | data formatting | bytes 262144 | tf_op jit(solution)/shard_map/reduce_sum | solution.py:55
  47.8 10.0 %collective-permute-start.4 = (f32[2,1,64,64]{3,2,0,1:T(8,128)S(1)}, f32[2,1,64,64]{3,2,0,1:T(8,128)S(1)}, u32[]{:S(2)}, u32[]{:S(2)}) collective-permute-start(f32[2,1,64,64]{3,2,0,1:T(8,128)S(1)} %bitcast_select_fusion.2), channel_id=1, source_target_pairs={{1,0},{2,1},{3,2},{4,3},{5,4},{6,5},{7,6},{8,7},{9,8},{10,9},{11,1... | collective-permute-start | bytes 98312 | tf_op jit(solution)/shard_map/ppermute | solution.py:24
  59.7 9.8 %reduce_sum.159 = f32[2,64,2,64,2]{4,3,2,1,0:T(8,128)} reshape(f32[2,128,128]{2,1,0:T(8,128)S(1)} %get-tuple-element.21) | data formatting | bytes 262144 | tf_op jit(solution)/shard_map/reduce_sum | solution.py:55
  100.2 5.7 %collective-permute-done.3 = f32[2,1,128,128]{3,2,1,0:T(8,128)S(1)} collective-permute-done((f32[2,1,128,128]{3,2,1,0:T(8,128)S(1)}, f32[2,1,128,128]{3,2,1,0:T(8,128)S(1)}, u32[]{:S(2)}, u32[]{:S(2)}) %collective-permute-start.3) | collective-permute-done | bytes 131104 | tf_op jit(solution)/shard_map/ppermute | solution.py:21
  106.8 10.0 %collective-permute-start.8 = (f32[2,1,128,128]{3,2,1,0:T(8,128)S(1)}, f32[2,1,128,128]{3,2,1,0:T(8,128)S(1)}, u32[]{:S(2)}, u32[]{:S(2)}) collective-permute-start(f32[2,1,128,128]{3,2,1,0:T(8,128)S(1)} %get-tuple-element.52), channel_id=1, source_target_pairs={{1,0},{2,1},{3,2},{4,3},{5,4},{6,5},{7,6},{8,7},{9,8},{10,9},{11,1... | collective-permute-start | bytes 393224 | tf_op jit(solution)/shard_map/ppermute | solution.py:24
  116.8 12.1 %collective-permute-start.9 = (f32[2,1,128,128]{3,2,1,0:T(8,128)S(1)}, f32[2,1,128,128]{3,2,1,0:T(8,128)S(1)}, u32[]{:S(2)}, u32[]{:S(2)}) collective-permute-start(f32[2,1,128,128]{3,2,1,0:T(8,128)S(1)} %get-tuple-element.51), channel_id=1, source_target_pairs={{0,1},{1,2},{2,3},{3,4},{4,5},{5,6},{6,7},{7,8},{8,9},{9,10},{10,1... | collective-permute-start | bytes 393224 | tf_op jit(solution)/shard_map/ppermute | solution.py:21
  129.1 9.8 %stack.166 = f32[1,1,2,64,2,64,2]{6,5,4,3,2,1,0:T(8,128)} reshape(f32[2,128,128]{2,1,0:T(8,128)S(1)} %get-tuple-element.36) | data formatting | bytes 262144 | tf_op jit(solution)/shard_map/stack | solution.py:48
  138.8 9.7 %stack.165 = f32[1,1,2,64,2,64,2]{6,5,4,3,2,1,0:T(8,128)} reshape(f32[2,128,128]{2,1,0:T(8,128)S(1)} %get-tuple-element.35) | data formatting | bytes 262144 | tf_op jit(solution)/shard_map/stack | solution.py:48
  160.2 9.8 %stack.169 = f32[1,1,2,64,2,64,2]{6,5,4,3,2,1,0:T(8,128)} reshape(f32[2,128,128]{2,1,0:T(8,128)S(1)} %get-tuple-element.34) | data formatting | bytes 262144 | tf_op jit(solution)/shard_map/stack | solution.py:48
  175.3 9.8 %stack.168 = f32[1,1,2,64,2,64,2]{6,5,4,3,2,1,0:T(8,128)} reshape(f32[2,128,128]{2,1,0:T(8,128)S(1)} %get-tuple-element.33) | data formatting | bytes 262144 | tf_op jit(solution)/shard_map/stack | solution.py:48
  216.0 10.2 %collective-permute-start.13 = (f32[2,1,64,64]{3,2,0,1:T(8,128)S(1)}, f32[2,1,64,64]{3,2,0,1:T(8,128)S(1)}, u32[]{:S(2)}, u32[]{:S(2)}) collective-permute-start(f32[2,1,64,64]{3,2,0,1:T(8,128)S(1)} %get-tuple-element.16), channel_id=1, source_target_pairs={{1,0},{2,1},{3,2},{4,3},{5,4},{6,5},{7,6},{8,7},{9,8},{10,9},{11,1... | collective-permute-start | bytes 98312 | tf_op jit(solution)/shard_map/ppermute | solution.py:24
  229.8 8.8 %collective-permute-start.15 = (f32[2,1,64,64]{3,2,0,1:T(8,128)S(1)}, f32[2,1,64,64]{3,2,0,1:T(8,128)S(1)}, u32[]{:S(2)}, u32[]{:S(2)}) collective-permute-start(f32[2,1,64,64]{3,2,0,1:T(8,128)S(1)} %get-tuple-element.18), channel_id=1, source_target_pairs={{1,0},{2,1},{3,2},{4,3},{5,4},{6,5},{7,6},{8,7},{9,8},{10,9},{11,1... | collective-permute-start | bytes 98312 | tf_op jit(solution)/shard_map/ppermute | solution.py:24
  240.5 9.8 %reduce_sum.164 = f32[2,64,2,64,2]{4,3,2,1,0:T(8,128)} reshape(f32[2,128,128]{2,1,0:T(8,128)S(1)} %get-tuple-element.19) | data formatting | bytes 262144 | tf_op jit(solution)/shard_map/reduce_sum | solution.py:55
  257.4 7.9 %collective-permute-done.17 = f32[2,2,128,128]{3,2,1,0:T(8,128)S(1)} collective-permute-done((f32[2,2,128,128]{3,2,1,0:T(8,128)S(1)}, f32[2,2,128,128]{3,2,1,0:T(8,128)S(1)}, u32[]{:S(2)}, u32[]{:S(2)}) %collective-permute-start.17) | collective-permute-done | bytes 262176 | tf_op jit(solution)/shard_map/ppermute | solution.py:32
  281.5 9.8 %reduce_sum.167 = f32[2,64,2,64,2]{4,3,2,1,0:T(8,128)} reshape(f32[2,128,128]{2,1,0:T(8,128)S(1)} %get-tuple-element.11) | data formatting | bytes 262144 | tf_op jit(solution)/shard_map/reduce_sum | solution.py:55
  297.2 9.7 %stack.188 = f32[1,1,2,64,2,64,2]{6,5,4,3,2,1,0:T(8,128)} reshape(f32[2,128,128]{2,1,0:T(8,128)S(1)} %get-tuple-element.32) | data formatting | bytes 262144 | tf_op jit(solution)/shard_map/stack | solution.py:48
  312.4 9.8 %stack.187 = f32[1,1,2,64,2,64,2]{6,5,4,3,2,1,0:T(8,128)} reshape(f32[2,128,128]{2,1,0:T(8,128)S(1)} %get-tuple-element.31) | data formatting | bytes 262144 | tf_op jit(solution)/shard_map/stack | solution.py:48
  322.1 6.1 %copy.27 = f32[1,1,2,64,2,64,2]{5,3,6,4,2,1,0:T(8,128)} copy(f32[1,1,2,64,2,64,2]{6,5,4,3,2,1,0:T(8,128)} %stack.187) | data formatting | bytes 262144 | tf_op jit(solution)/shard_map/stack | solution.py:48
  331.3 9.8 %reduce_sum.170 = f32[2,64,2,64,2]{4,3,2,1,0:T(8,128)} reshape(f32[2,128,128]{2,1,0:T(8,128)S(1)} %get-tuple-element.13) | data formatting | bytes 262144 | tf_op jit(solution)/shard_map/reduce_sum | solution.py:55
  345.6 7.3 %collective-permute-start.24 = (f32[2,2,1,64,64]{4,3,1,2,0:T(8,128)S(1)}, f32[2,2,1,64,64]{4,3,1,2,0:T(8,128)S(1)}, u32[]{:S(2)}, u32[]{:S(2)}) collective-permute-start(f32[2,2,1,64,64]{4,3,1,2,0:T(8,128)S(1)} %pad_maximum_fusion.26), channel_id=1, source_target_pairs={{1,0},{2,1},{3,2},{4,3},{5,4},{6,5},{7,6},{8,7},{9,8},{10,9},{11,1... | collective-permute-start | bytes 196616 | tf_op jit(solution)/shard_map/ppermute | solution.py:24
  354.9 8.2 %collective-permute-start.22 = (f32[2,1,128,128]{3,2,1,0:T(8,128)S(1)}, f32[2,1,128,128]{3,2,1,0:T(8,128)S(1)}, u32[]{:S(2)}, u32[]{:S(2)}) collective-permute-start(f32[2,1,128,128]{3,2,1,0:T(8,128)S(1)} %get-tuple-element.44), channel_id=1, source_target_pairs={{1,0},{2,1},{3,2},{4,3},{5,4},{6,5},{7,6},{8,7},{9,8},{10,9},{11,1... | collective-permute-start | bytes 393224 | tf_op jit(solution)/shard_map/ppermute | solution.py:24
  365.8 6.3 %collective-permute-done.23 = f32[2,1,128,128]{3,2,1,0:T(8,128)S(1)} collective-permute-done((f32[2,1,128,128]{3,2,1,0:T(8,128)S(1)}, f32[2,1,128,128]{3,2,1,0:T(8,128)S(1)}, u32[]{:S(2)}, u32[]{:S(2)}) %collective-permute-start.23) | collective-permute-done | bytes 131104 | tf_op jit(solution)/shard_map/ppermute | solution.py:21
  372.9 10.0 %collective-permute-start.26 = (f32[2,1,128,128]{3,2,1,0:T(8,128)S(1)}, f32[2,1,128,128]{3,2,1,0:T(8,128)S(1)}, u32[]{:S(2)}, u32[]{:S(2)}) collective-permute-start(f32[2,1,128,128]{3,2,1,0:T(8,128)S(1)} %get-tuple-element.42), channel_id=1, source_target_pairs={{1,0},{2,1},{3,2},{4,3},{5,4},{6,5},{7,6},{8,7},{9,8},{10,9},{11,1... | collective-permute-start | bytes 393224 | tf_op jit(solution)/shard_map/ppermute | solution.py:24
  384.9 9.8 %stack.191 = f32[1,1,2,64,2,64,2]{6,5,4,3,2,1,0:T(8,128)} reshape(f32[2,128,128]{2,1,0:T(8,128)S(1)} %get-tuple-element.30) | data formatting | bytes 262144 | tf_op jit(solution)/shard_map/stack | solution.py:48
  394.6 9.7 %stack.190 = f32[1,1,2,64,2,64,2]{6,5,4,3,2,1,0:T(8,128)} reshape(f32[2,128,128]{2,1,0:T(8,128)S(1)} %get-tuple-element.29) | data formatting | bytes 262144 | tf_op jit(solution)/shard_map/stack | solution.py:48
  415.9 9.8 %stack.194 = f32[1,1,2,64,2,64,2]{6,5,4,3,2,1,0:T(8,128)} reshape(f32[2,128,128]{2,1,0:T(8,128)S(1)} %get-tuple-element.28) | data formatting | bytes 262144 | tf_op jit(solution)/shard_map/stack | solution.py:48
  431.1 9.8 %stack.193 = f32[1,1,2,64,2,64,2]{6,5,4,3,2,1,0:T(8,128)} reshape(f32[2,128,128]{2,1,0:T(8,128)S(1)} %get-tuple-element.27) | data formatting | bytes 262144 | tf_op jit(solution)/shard_map/stack | solution.py:48
  463.6 10.2 %collective-permute-start.31 = (f32[2,1,64,64]{3,2,0,1:T(8,128)S(1)}, f32[2,1,64,64]{3,2,0,1:T(8,128)S(1)}, u32[]{:S(2)}, u32[]{:S(2)}) collective-permute-start(f32[2,1,64,64]{3,2,0,1:T(8,128)S(1)} %bitcast_select_fusion), channel_id=1, source_target_pairs={{1,0},{2,1},{3,2},{4,3},{5,4},{6,5},{7,6},{8,7},{9,8},{10,9},{11,1... | collective-permute-start | bytes 98312 | tf_op jit(solution)/shard_map/ppermute | solution.py:24
  477.4 8.8 %collective-permute-start.33 = (f32[2,1,64,64]{3,2,0,1:T(8,128)S(1)}, f32[2,1,64,64]{3,2,0,1:T(8,128)S(1)}, u32[]{:S(2)}, u32[]{:S(2)}) collective-permute-start(f32[2,1,64,64]{3,2,0,1:T(8,128)S(1)} %fusion.134), channel_id=1, source_target_pairs={{1,0},{2,1},{3,2},{4,3},{5,4},{6,5},{7,6},{8,7},{9,8},{10,9},{11,1... | collective-permute-start | bytes 98312 | tf_op jit(solution)/shard_map/ppermute | solution.py:24
  488.3 9.8 %reduce_sum.175 = f32[2,64,2,64,2]{4,3,2,1,0:T(8,128)} reshape(f32[2,128,128]{2,1,0:T(8,128)S(1)} %get-tuple-element.9) | data formatting | bytes 262144 | tf_op jit(solution)/shard_map/reduce_sum | solution.py:55
  (190 shorter events, 205.7 us)
Async XLA Ops:
  1.0 7.8 %collective-permute-start = (f32[2,1,128,128]{3,2,1,0:T(8,128)S(1)}, f32[2,1,128,128]{3,2,1,0:T(8,128)S(1)}, u32[]{:S(2)}, u32[]{:S(2)}) collective-permute-start(f32[2,1,128,128]{3,2,1,0:T(8,128)S(1)} %get-tuple-element.56), channel_id=1, source_target_pairs={{1,0},{2,1},{3,2},{4,3},{5,4},{6,5},{7,6},{8,7},{9,8},{10,9},{11,1... | collective-permute-start | bytes 393224 | tf_op jit(solution)/shard_map/ppermute | solution.py:24
  3.6 8.0 %collective-permute-start.1 = (f32[2,1,128,128]{3,2,1,0:T(8,128)S(1)}, f32[2,1,128,128]{3,2,1,0:T(8,128)S(1)}, u32[]{:S(2)}, u32[]{:S(2)}) collective-permute-start(f32[2,1,128,128]{3,2,1,0:T(8,128)S(1)} %get-tuple-element.55), channel_id=1, source_target_pairs={{0,1},{1,2},{2,3},{3,4},{4,5},{5,6},{6,7},{7,8},{8,9},{9,10},{10,1... | collective-permute-start | bytes 393224 | tf_op jit(solution)/shard_map/ppermute | solution.py:21
  47.8 49.2 %collective-permute-start.4 = (f32[2,1,64,64]{3,2,0,1:T(8,128)S(1)}, f32[2,1,64,64]{3,2,0,1:T(8,128)S(1)}, u32[]{:S(2)}, u32[]{:S(2)}) collective-permute-start(f32[2,1,64,64]{3,2,0,1:T(8,128)S(1)} %bitcast_select_fusion.2), channel_id=1, source_target_pairs={{1,0},{2,1},{3,2},{4,3},{5,4},{6,5},{7,6},{8,7},{9,8},{10,9},{11,1... | collective-permute-start | bytes 98312 | tf_op jit(solution)/shard_map/ppermute | solution.py:24
  57.7 41.4 %collective-permute-start.5 = (f32[2,1,64,64]{3,2,0,1:T(8,128)S(1)}, f32[2,1,64,64]{3,2,0,1:T(8,128)S(1)}, u32[]{:S(2)}, u32[]{:S(2)}) collective-permute-start(f32[2,1,64,64]{3,2,0,1:T(8,128)S(1)} %bitcast_select_fusion.2), channel_id=1, source_target_pairs={{0,1},{1,2},{2,3},{3,4},{4,5},{5,6},{6,7},{7,8},{8,9},{9,10},{10,1... | collective-permute-start | bytes 98312 | tf_op jit(solution)/shard_map/ppermute | solution.py:21
  74.0 26.0 %collective-permute-start.6 = (f32[2,2,1,64,64]{4,3,1,2,0:T(8,128)S(1)}, f32[2,2,1,64,64]{4,3,1,2,0:T(8,128)S(1)}, u32[]{:S(2)}, u32[]{:S(2)}) collective-permute-start(f32[2,2,1,64,64]{4,3,1,2,0:T(8,128)S(1)} %pad_maximum_fusion.25), channel_id=1, source_target_pairs={{1,0},{2,1},{3,2},{4,3},{5,4},{6,5},{7,6},{8,7},{9,8},{10,9},{11,1... | collective-permute-start | bytes 196616 | tf_op jit(solution)/shard_map/ppermute | solution.py:24
  76.4 23.6 %collective-permute-start.7 = (f32[2,2,1,64,64]{4,3,1,2,0:T(8,128)S(1)}, f32[2,2,1,64,64]{4,3,1,2,0:T(8,128)S(1)}, u32[]{:S(2)}, u32[]{:S(2)}) collective-permute-start(f32[2,2,1,64,64]{4,3,1,2,0:T(8,128)S(1)} %pad_maximum_fusion.25), channel_id=1, source_target_pairs={{0,1},{1,2},{2,3},{3,4},{4,5},{5,6},{6,7},{7,8},{8,9},{9,10},{10,1... | collective-permute-start | bytes 196616 | tf_op jit(solution)/shard_map/ppermute | solution.py:21
  81.1 19.1 %collective-permute-start.2 = (f32[2,1,128,128]{3,2,1,0:T(8,128)S(1)}, f32[2,1,128,128]{3,2,1,0:T(8,128)S(1)}, u32[]{:S(2)}, u32[]{:S(2)}) collective-permute-start(f32[2,1,128,128]{3,2,1,0:T(8,128)S(1)} %get-tuple-element.54), channel_id=1, source_target_pairs={{1,0},{2,1},{3,2},{4,3},{5,4},{6,5},{7,6},{8,7},{9,8},{10,9},{11,1... | collective-permute-start | bytes 393224 | tf_op jit(solution)/shard_map/ppermute | solution.py:24
  97.0 9.0 %collective-permute-start.3 = (f32[2,1,128,128]{3,2,1,0:T(8,128)S(1)}, f32[2,1,128,128]{3,2,1,0:T(8,128)S(1)}, u32[]{:S(2)}, u32[]{:S(2)}) collective-permute-start(f32[2,1,128,128]{3,2,1,0:T(8,128)S(1)} %get-tuple-element.53), channel_id=1, source_target_pairs={{0,1},{1,2},{2,3},{3,4},{4,5},{5,6},{6,7},{7,8},{8,9},{9,10},{10,1... | collective-permute-start | bytes 393224 | tf_op jit(solution)/shard_map/ppermute | solution.py:21
  106.8 52.6 %collective-permute-start.8 = (f32[2,1,128,128]{3,2,1,0:T(8,128)S(1)}, f32[2,1,128,128]{3,2,1,0:T(8,128)S(1)}, u32[]{:S(2)}, u32[]{:S(2)}) collective-permute-start(f32[2,1,128,128]{3,2,1,0:T(8,128)S(1)} %get-tuple-element.52), channel_id=1, source_target_pairs={{1,0},{2,1},{3,2},{4,3},{5,4},{6,5},{7,6},{8,7},{9,8},{10,9},{11,1... | collective-permute-start | bytes 393224 | tf_op jit(solution)/shard_map/ppermute | solution.py:24
  116.8 42.7 %collective-permute-start.9 = (f32[2,1,128,128]{3,2,1,0:T(8,128)S(1)}, f32[2,1,128,128]{3,2,1,0:T(8,128)S(1)}, u32[]{:S(2)}, u32[]{:S(2)}) collective-permute-start(f32[2,1,128,128]{3,2,1,0:T(8,128)S(1)} %get-tuple-element.51), channel_id=1, source_target_pairs={{0,1},{1,2},{2,3},{3,4},{4,5},{5,6},{6,7},{7,8},{8,9},{9,10},{10,1... | collective-permute-start | bytes 393224 | tf_op jit(solution)/shard_map/ppermute | solution.py:21
  199.6 7.1 %collective-permute-start.10 = (f32[2,1,64,64]{3,2,0,1:T(8,128)S(1)}, f32[2,1,64,64]{3,2,0,1:T(8,128)S(1)}, u32[]{:S(2)}, u32[]{:S(2)}) collective-permute-start(f32[2,1,64,64]{3,2,0,1:T(8,128)S(1)} %bitcast_add_fusion.3), channel_id=1, source_target_pairs={{1,0},{2,1},{3,2},{4,3},{5,4},{6,5},{7,6},{8,7},{9,8},{10,9},{11,1... | collective-permute-start | bytes 98312 | tf_op jit(solution)/shard_map/ppermute | solution.py:24
  202.0 8.4 %collective-permute-start.11 = (f32[2,1,64,64]{3,2,0,1:T(8,128)S(1)}, f32[2,1,64,64]{3,2,0,1:T(8,128)S(1)}, u32[]{:S(2)}, u32[]{:S(2)}) collective-permute-start(f32[2,1,64,64]{3,2,0,1:T(8,128)S(1)} %bitcast_add_fusion.3), channel_id=1, source_target_pairs={{0,1},{1,2},{2,3},{3,4},{4,5},{5,6},{6,7},{7,8},{8,9},{9,10},{10,1... | collective-permute-start | bytes 98312 | tf_op jit(solution)/shard_map/ppermute | solution.py:21
  210.7 5.3 %collective-permute-start.12 = (f32[2,1,64,64]{3,2,0,1:T(8,128)S(1)}, f32[2,1,64,64]{3,2,0,1:T(8,128)S(1)}, u32[]{:S(2)}, u32[]{:S(2)}) collective-permute-start(f32[2,1,64,64]{3,2,0,1:T(8,128)S(1)} %fusion.120), channel_id=1, source_target_pairs={{0,64},{1,65},{2,66},{3,67},{4,68},{5,69},{6,70},{7,71},{8,72},{9,... | collective-permute-start | bytes 98312 | tf_op jit(solution)/shard_map/ppermute | solution.py:32
  216.0 12.1 %collective-permute-start.13 = (f32[2,1,64,64]{3,2,0,1:T(8,128)S(1)}, f32[2,1,64,64]{3,2,0,1:T(8,128)S(1)}, u32[]{:S(2)}, u32[]{:S(2)}) collective-permute-start(f32[2,1,64,64]{3,2,0,1:T(8,128)S(1)} %get-tuple-element.16), channel_id=1, source_target_pairs={{1,0},{2,1},{3,2},{4,3},{5,4},{6,5},{7,6},{8,7},{9,8},{10,9},{11,1... | collective-permute-start | bytes 98312 | tf_op jit(solution)/shard_map/ppermute | solution.py:24
  229.8 25.6 %collective-permute-start.15 = (f32[2,1,64,64]{3,2,0,1:T(8,128)S(1)}, f32[2,1,64,64]{3,2,0,1:T(8,128)S(1)}, u32[]{:S(2)}, u32[]{:S(2)}) collective-permute-start(f32[2,1,64,64]{3,2,0,1:T(8,128)S(1)} %get-tuple-element.18), channel_id=1, source_target_pairs={{1,0},{2,1},{3,2},{4,3},{5,4},{6,5},{7,6},{8,7},{9,8},{10,9},{11,1... | collective-permute-start | bytes 98312 | tf_op jit(solution)/shard_map/ppermute | solution.py:24
  238.6 16.8 %collective-permute-start.16 = (f32[2,1,64,64]{3,2,0,1:T(8,128)S(1)}, f32[2,1,64,64]{3,2,0,1:T(8,128)S(1)}, u32[]{:S(2)}, u32[]{:S(2)}) collective-permute-start(f32[2,1,64,64]{3,2,0,1:T(8,128)S(1)} %get-tuple-element.18), channel_id=1, source_target_pairs={{0,1},{1,2},{2,3},{3,4},{4,5},{5,6},{6,7},{7,8},{8,9},{9,10},{10,1... | collective-permute-start | bytes 98312 | tf_op jit(solution)/shard_map/ppermute | solution.py:21
  256.1 9.3 %collective-permute-start.17 = (f32[2,2,128,128]{3,2,1,0:T(8,128)S(1)}, f32[2,2,128,128]{3,2,1,0:T(8,128)S(1)}, u32[]{:S(2)}, u32[]{:S(2)}) collective-permute-start(f32[2,2,128,128]{3,2,1,0:T(8,128)S(1)} %broadcast_add_fusion), channel_id=1, source_target_pairs={{0,64},{1,65},{2,66},{3,67},{4,68},{5,69},{6,70},{7,71},{8,72},{9,... | collective-permute-start | bytes 786440 | tf_op jit(solution)/shard_map/ppermute | solution.py:32
  266.5 61.7 %collective-permute-start.20 = (f32[3,2,1,128,128]{4,3,2,1,0:T(8,128)}, f32[3,2,1,128,128]{4,3,2,1,0:T(8,128)S(1)}, u32[]{:S(2)}, u32[]{:S(2)}) collective-permute-start(f32[3,2,1,128,128]{4,3,2,1,0:T(8,128)} %get-tuple-element.26), channel_id=1, source_target_pairs={{1,0},{2,1},{3,2},{4,3},{5,4},{6,5},{7,6},{8,7},{9,8},{10,9},{11,1... | collective-permute-start | bytes 1179656 | tf_op jit(solution)/shard_map/ppermute | solution.py:24
  269.7 58.5 %collective-permute-start.21 = (f32[3,2,1,128,128]{4,3,2,1,0:T(8,128)}, f32[3,2,1,128,128]{4,3,2,1,0:T(8,128)S(1)}, u32[]{:S(2)}, u32[]{:S(2)}) collective-permute-start(f32[3,2,1,128,128]{4,3,2,1,0:T(8,128)} %get-tuple-element.25), channel_id=1, source_target_pairs={{0,1},{1,2},{2,3},{3,4},{4,5},{5,6},{6,7},{7,8},{8,9},{9,10},{10,1... | collective-permute-start | bytes 1179656 | tf_op jit(solution)/shard_map/ppermute | solution.py:21
  274.2 21.6 %collective-permute-start.18 = (f32[2,1,128,128]{3,2,1,0:T(8,128)}, f32[2,1,128,128]{3,2,1,0:T(8,128)S(1)}, u32[]{:S(2)}, u32[]{:S(2)}) collective-permute-start(f32[2,1,128,128]{3,2,1,0:T(8,128)} %get-tuple-element.46), channel_id=1, source_target_pairs={{1,0},{2,1},{3,2},{4,3},{5,4},{6,5},{7,6},{8,7},{9,8},{10,9},{11,1... | collective-permute-start | bytes 393224 | tf_op jit(solution)/shard_map/ppermute | solution.py:24
  278.6 17.3 %collective-permute-start.19 = (f32[2,1,128,128]{3,2,1,0:T(8,128)S(1)}, f32[2,1,128,128]{3,2,1,0:T(8,128)S(1)}, u32[]{:S(2)}, u32[]{:S(2)}) collective-permute-start(f32[2,1,128,128]{3,2,1,0:T(8,128)S(1)} %get-tuple-element.45), channel_id=1, source_target_pairs={{0,1},{1,2},{2,3},{3,4},{4,5},{5,6},{6,7},{7,8},{8,9},{9,10},{10,1... | collective-permute-start | bytes 393224 | tf_op jit(solution)/shard_map/ppermute | solution.py:21
  345.6 19.8 %collective-permute-start.24 = (f32[2,2,1,64,64]{4,3,1,2,0:T(8,128)S(1)}, f32[2,2,1,64,64]{4,3,1,2,0:T(8,128)S(1)}, u32[]{:S(2)}, u32[]{:S(2)}) collective-permute-start(f32[2,2,1,64,64]{4,3,1,2,0:T(8,128)S(1)} %pad_maximum_fusion.26), channel_id=1, source_target_pairs={{1,0},{2,1},{3,2},{4,3},{5,4},{6,5},{7,6},{8,7},{9,8},{10,9},{11,1... | collective-permute-start | bytes 196616 | tf_op jit(solution)/shard_map/ppermute | solution.py:24
  353.0 12.5 %collective-permute-start.25 = (f32[2,2,1,64,64]{4,3,1,2,0:T(8,128)S(1)}, f32[2,2,1,64,64]{4,3,1,2,0:T(8,128)S(1)}, u32[]{:S(2)}, u32[]{:S(2)}) collective-permute-start(f32[2,2,1,64,64]{4,3,1,2,0:T(8,128)S(1)} %pad_maximum_fusion.26), channel_id=1, source_target_pairs={{0,1},{1,2},{2,3},{3,4},{4,5},{5,6},{6,7},{7,8},{8,9},{9,10},{10,1... | collective-permute-start | bytes 196616 | tf_op jit(solution)/shard_map/ppermute | solution.py:21
  354.9 10.9 %collective-permute-start.22 = (f32[2,1,128,128]{3,2,1,0:T(8,128)S(1)}, f32[2,1,128,128]{3,2,1,0:T(8,128)S(1)}, u32[]{:S(2)}, u32[]{:S(2)}) collective-permute-start(f32[2,1,128,128]{3,2,1,0:T(8,128)S(1)} %get-tuple-element.44), channel_id=1, source_target_pairs={{1,0},{2,1},{3,2},{4,3},{5,4},{6,5},{7,6},{8,7},{9,8},{10,9},{11,1... | collective-permute-start | bytes 393224 | tf_op jit(solution)/shard_map/ppermute | solution.py:24
  363.1 9.0 %collective-permute-start.23 = (f32[2,1,128,128]{3,2,1,0:T(8,128)S(1)}, f32[2,1,128,128]{3,2,1,0:T(8,128)S(1)}, u32[]{:S(2)}, u32[]{:S(2)}) collective-permute-start(f32[2,1,128,128]{3,2,1,0:T(8,128)S(1)} %get-tuple-element.43), channel_id=1, source_target_pairs={{0,1},{1,2},{2,3},{3,4},{4,5},{5,6},{6,7},{7,8},{8,9},{9,10},{10,1... | collective-permute-start | bytes 393224 | tf_op jit(solution)/shard_map/ppermute | solution.py:21
  372.9 42.3 %collective-permute-start.26 = (f32[2,1,128,128]{3,2,1,0:T(8,128)S(1)}, f32[2,1,128,128]{3,2,1,0:T(8,128)S(1)}, u32[]{:S(2)}, u32[]{:S(2)}) collective-permute-start(f32[2,1,128,128]{3,2,1,0:T(8,128)S(1)} %get-tuple-element.42), channel_id=1, source_target_pairs={{1,0},{2,1},{3,2},{4,3},{5,4},{6,5},{7,6},{8,7},{9,8},{10,9},{11,1... | collective-permute-start | bytes 393224 | tf_op jit(solution)/shard_map/ppermute | solution.py:24
  382.9 32.3 %collective-permute-start.27 = (f32[2,1,128,128]{3,2,1,0:T(8,128)S(1)}, f32[2,1,128,128]{3,2,1,0:T(8,128)S(1)}, u32[]{:S(2)}, u32[]{:S(2)}) collective-permute-start(f32[2,1,128,128]{3,2,1,0:T(8,128)S(1)} %get-tuple-element.41), channel_id=1, source_target_pairs={{0,1},{1,2},{2,3},{3,4},{4,5},{5,6},{6,7},{7,8},{8,9},{9,10},{10,1... | collective-permute-start | bytes 393224 | tf_op jit(solution)/shard_map/ppermute | solution.py:21
  447.2 7.1 %collective-permute-start.28 = (f32[2,1,64,64]{3,2,0,1:T(8,128)S(1)}, f32[2,1,64,64]{3,2,0,1:T(8,128)S(1)}, u32[]{:S(2)}, u32[]{:S(2)}) collective-permute-start(f32[2,1,64,64]{3,2,0,1:T(8,128)S(1)} %bitcast_add_fusion.2), channel_id=1, source_target_pairs={{1,0},{2,1},{3,2},{4,3},{5,4},{6,5},{7,6},{8,7},{9,8},{10,9},{11,1... | collective-permute-start | bytes 98312 | tf_op jit(solution)/shard_map/ppermute | solution.py:24
  449.6 8.4 %collective-permute-start.29 = (f32[2,1,64,64]{3,2,0,1:T(8,128)S(1)}, f32[2,1,64,64]{3,2,0,1:T(8,128)S(1)}, u32[]{:S(2)}, u32[]{:S(2)}) collective-permute-start(f32[2,1,64,64]{3,2,0,1:T(8,128)S(1)} %bitcast_add_fusion.2), channel_id=1, source_target_pairs={{0,1},{1,2},{2,3},{3,4},{4,5},{5,6},{6,7},{7,8},{8,9},{9,10},{10,1... | collective-permute-start | bytes 98312 | tf_op jit(solution)/shard_map/ppermute | solution.py:21
  463.6 12.1 %collective-permute-start.31 = (f32[2,1,64,64]{3,2,0,1:T(8,128)S(1)}, f32[2,1,64,64]{3,2,0,1:T(8,128)S(1)}, u32[]{:S(2)}, u32[]{:S(2)}) collective-permute-start(f32[2,1,64,64]{3,2,0,1:T(8,128)S(1)} %bitcast_select_fusion), channel_id=1, source_target_pairs={{1,0},{2,1},{3,2},{4,3},{5,4},{6,5},{7,6},{8,7},{9,8},{10,9},{11,1... | collective-permute-start | bytes 98312 | tf_op jit(solution)/shard_map/ppermute | solution.py:24
  477.4 25.2 %collective-permute-start.33 = (f32[2,1,64,64]{3,2,0,1:T(8,128)S(1)}, f32[2,1,64,64]{3,2,0,1:T(8,128)S(1)}, u32[]{:S(2)}, u32[]{:S(2)}) collective-permute-start(f32[2,1,64,64]{3,2,0,1:T(8,128)S(1)} %fusion.134), channel_id=1, source_target_pairs={{1,0},{2,1},{3,2},{4,3},{5,4},{6,5},{7,6},{8,7},{9,8},{10,9},{11,1... | collective-permute-start | bytes 98312 | tf_op jit(solution)/shard_map/ppermute | solution.py:24
  486.2 16.4 %collective-permute-start.34 = (f32[2,1,64,64]{3,2,0,1:T(8,128)S(1)}, f32[2,1,64,64]{3,2,0,1:T(8,128)S(1)}, u32[]{:S(2)}, u32[]{:S(2)}) collective-permute-start(f32[2,1,64,64]{3,2,0,1:T(8,128)S(1)} %fusion.134), channel_id=1, source_target_pairs={{0,1},{1,2},{2,3},{3,4},{4,5},{5,6},{6,7},{7,8},{8,9},{9,10},{10,1... | collective-permute-start | bytes 98312 | tf_op jit(solution)/shard_map/ppermute | solution.py:21
  (10 other events, 36.2 us)
where the time goes:
time: 514 us; the launch traced here: 504 us
  local copies, waits for them, and re-layouts  252 us (49%)
  starting transfers between devices  165 us (32%)
  other arithmetic  44.1 us (9%)
  waiting for transfers between devices  41.5 us (8%)
    another operation x24, local copies, waits for them, and re-layouts, react(): return jnp.stack([rate_a, rate_b], axis=-4)  183 us
    ppermute x16, starting transfers between devices, padded_2(): lax.ppermute(lax.slice_in_dim(block, 0, width, axis=dim), axis, backward)  106 us
    reduce_sum x7, local copies, waits for them, and re-layouts, restrict(): return 0.125 * jnp.sum(blocks, axis=(-5, -3, -1))  64.1 us
    ppermute x16, starting transfers between devices, padded_2(): lax.ppermute(lax.slice_in_dim(block, block.shape[dim] - width, None, axis...  55.4 us
    reduce_sum x14, other arithmetic, restrict(): return 0.125 * jnp.sum(blocks, axis=(-5, -3, -1))  31.1 us
    ppermute x16, waiting for transfers between devices, padded_2(): lax.ppermute(lax.slice_in_dim(block, block.shape[dim] - width, None, axis...  24.8 us
    ppermute x3, waiting for transfers between devices, passed_along(): lax.ppermute(value, axis, [(source, source + steps) for source in range(f...  15.9 us
  transfers between devices with their start and end apart: 35, of which 11 were waited for; matrix products, arithmetic and copies ran while one was open for 33% of the time, Pallas kernels for 0%

commit v1 on v0

v1 whole, which is shorter than its diff:
```python
import functools

import jax
import jax.numpy as jnp
from jax import lax
from jax.experimental import pallas as pl
from jax.experimental.pallas import tpu as pltpu
from jax.sharding import PartitionSpec as P

MESH = pl.DeviceIdType.MESH
F32 = jnp.float32
STEP = 0.25
HALF = 0.125
FEED = 0.04
KILL = 0.06
S0 = (STEP * 5.0 / 24.0, STEP / 3.0, -STEP / 24.0)
S1 = (-STEP / 24.0, STEP / 3.0, STEP * 5.0 / 24.0)
N_COPIES = 48


def iota(dim):
    return lax.broadcasted_iota(jnp.int32, (64, 128), dim)


def even_lane():
    return iota(1) % 2 == 0


def beside_lanes(x, by):
    lane = iota(1)
    low = jnp.where(lane < by, 0.0, pltpu.roll(x, by, 1))
    high = jnp.where(lane >= 128 - by, 0.0, pltpu.roll(x, 128 - by, 1))
    return low + high


def row_above(x):
    return jnp.where(iota(0) == 0, 0.0, pltpu.roll(x, 1, 0))


def row_below(x):
    return jnp.where(iota(0) == 63, 0.0, pltpu.roll(x, 63, 0))


def fine_rate(buf, kn, p):
    centre = [[buf[p, sp, par] for par in range(2)] for sp in range(2)]
    kappa = [kn[p - 1, pl.ds(par, 64, stride=2), :] for par in range(2)]
    lap = []
    for sp in range(2):
        e, o = centre[sp]
        le = buf[p - 1, sp, 0] + buf[p + 1, sp, 0] + o + row_above(o) + beside_lanes(e, 1) - 6.0 * e
        lo = buf[p - 1, sp, 1] + buf[p + 1, sp, 1] + e + row_below(e) + beside_lanes(o, 1) - 6.0 * o
        lap.append((le, lo))
    out = [[None, None], [None, None]]
    for par in range(2):
        u, v = centre[0][par], centre[1][par]
        r = u * v * v
        out[0][par] = kappa[par] * lap[0][par] - r + FEED * (1.0 - u)
        out[1][par] = (0.5 * kappa[par]) * lap[1][par] + r - (FEED + KILL) * v
    return out


def each():
    return [(sp, par) for sp in range(2) for par in range(2)]


def pairs(su, sv):
    return jnp.where(even_lane(), su + pltpu.roll(su, 127, 1), sv + pltpu.roll(sv, 1, 1))


def restrict(buf, a, b):
    s = [buf[a, sp, 0] + buf[a, sp, 1] + buf[b, sp, 0] + buf[b, sp, 1] for sp in range(2)]
    return 0.125 * pairs(s[0], s[1])


def prolong(d):
    even = even_lane()
    return jnp.where(even, d, pltpu.roll(d, 1, 1)), jnp.where(even, pltpu.roll(d, 127, 1), d)


def local_rate(c):
    even = even_lane()
    u, v = prolong(c)
    r = u * v * v
    return jnp.where(even, -r, r) - jnp.where(even, FEED, FEED + KILL) * c


def coarse_lap(below, d, above):
    return below + above + row_above(d) + row_below(d) + beside_lanes(d, 2) - 6.0 * d


def kernel(
    n, init_ref, kap_ref, out_ref,
    nat, kn, x0, x1, x2, f0, tq0, tq1, u0, u1, u2, y, base, g0, ex, v1p, v2p,
    d1c, b2c, kc, wi, wpk, d11c, b11c, dd0, dd1, dd2, ddy, d5, c5, c5own, w0p, a1p, w1p,
    lsem, ssem, rsem,
):
    me = lax.axis_index("space")
    t = lax.axis_index("tm")
    c = lax.rem(me, 2)
    partner = me + 1 - 2 * c
    outer = me - 1 + 2 * c
    far_in = me + 2 - 4 * c
    far_out = me - 2 + 4 * c
    has_out = jnp.logical_and(outer >= 0, outer < n)
    has_far = jnp.logical_and(far_in >= 0, far_in < n)
    always = None
    first, second = t == 0, t == 1
    m_out = jnp.where(has_out, 1.0, 0.0).astype(F32)

    def when(cond, fn):
        if cond is None:
            fn()
        else:
            pl.when(cond)(fn)

    def both(a, b):
        if a is None:
            return b
        return a if b is None else jnp.logical_and(a, b)

    copies = []

    def copy(src, dst, tm, space, cond, back="same"):
        i = len(copies)
        cp = pltpu.make_async_remote_copy(
            src_ref=src, dst_ref=dst, send_sem=ssem.at[i], recv_sem=rsem.at[i],
            device_id=(tm, space), device_id_type=MESH)
        copies.append((cond, cp))
        return cond, cond if isinstance(back, str) else back, cp

    def start(*cs):
        for cond, _, cp in cs:
            when(cond, cp.start)

    def arrived(*cs):
        for _, back, cp in cs:
            when(back, cp.wait_recv)

    locals_ = [
        pltpu.make_async_copy(init_ref.at[:, 1 - c], nat.at[1], lsem.at[0]),
        pltpu.make_async_copy(init_ref.at[:, c], nat.at[2], lsem.at[1]),
        pltpu.make_async_copy(kap_ref.at[1 - c], kn.at[0], lsem.at[2]),
        pltpu.make_async_copy(kap_ref.at[c], kn.at[1], lsem.at[3]),
    ]
    for cp in locals_:
        cp.start()

    barrier = pltpu.get_barrier_semaphore()
    around = [(always, partner), (has_out, outer), (has_far, far_in), (has_out, far_out)]
    greet = [(t, cond, s) for cond, s in around] + [(1 - t, cond, s) for cond, s in [(always, me)] + around]
    for tm, cond, s in greet:
        when(cond, lambda tm=tm, s=s: pl.semaphore_signal(barrier, inc=1, device_id=(tm, s), device_id_type=MESH))

    @pl.when(jnp.logical_not(has_out))
    def _():
        zero_plane = jnp.zeros((2, 2, 64, 128), F32)
        for buf in (x1, x2):
            buf[4] = zero_plane
        v2p[3] = zero_plane
        nat[3] = jnp.zeros((2, 128, 128), F32)
        nat[4] = jnp.zeros((2, 128, 128), F32)
        kn[2] = jnp.zeros((128, 128), F32)
        zero = jnp.zeros((64, 128), F32)
        for buf in (d1c, d11c, c5, w0p):
            buf[3] = zero
            buf[4] = zero
        for buf in (b2c, kc, b11c, d5, a1p, w1p):
            buf[2] = zero

    @pl.when(jnp.logical_not(has_far))
    def _():
        zero = jnp.zeros((64, 128), F32)
        for buf in (d1c, d11c, c5, w0p):
            buf[0] = zero

    pl.semaphore_wait(barrier, 3 + 4 * has_out.astype(jnp.int32) + 2 * has_far.astype(jnp.int32))

    p_init = copy(init_ref.at[:, 1 - c], nat.at[0], t, partner, always)
    o_init = copy(init_ref.at[:, c], nat.at[3], t, outer, has_out)
    o_kap = copy(kap_ref.at[c], kn.at[2], t, outer, has_out)
    o_init2 = copy(init_ref.at[:, 1 - c], nat.at[4], t, outer, has_out)
    start(p_init, o_init, o_kap, o_init2)

    def convert(p):
        for sp, par in each():
            x0[p, sp, par] = nat[p, sp, pl.ds(par, 64, stride=2), :]

    for cp in locals_:
        cp.wait()
    convert(1)
    convert(2)
    ks = (kn[0, pl.ds(0, 64, stride=2), :] + kn[0, pl.ds(1, 64, stride=2), :]
          + kn[1, pl.ds(0, 64, stride=2), :] + kn[1, pl.ds(1, 64, stride=2), :])
    kc[1] = (0.125 * HALF / 4.0) * pairs(ks, 0.5 * ks)
    p_kc = copy(kc.at[1], kc.at[0], t, partner, always)
    o_kc = copy(kc.at[1], kc.at[2], t, outer, has_out)

    def masked(p):
        return jnp.where(p == 3, m_out, 1.0).astype(F32)

    def loop(lo, hi, body):
        def step(i, carry):
            body(i)
            return carry
        lax.fori_loop(lo, hi, step, 0)

    p_v1 = copy(x1.at[1], x1.at[0], t, partner, always)
    o_v1 = copy(x1.at[1], x1.at[4], t, outer, has_out)
    p_v2 = copy(x2.at[1], x2.at[0], t, partner, always)
    o_v2 = copy(x2.at[1], x2.at[4], t, outer, has_out)

    arrived(p_init)
    convert(0)

    def body_a1(p):
        @pl.when(p == 2)
        def _():
            arrived(o_init, o_kap, o_init2)
            convert(3)
            convert(4)

        f = fine_rate(x0, kn, p)
        m = masked(p)
        for sp, par in each():
            f0[p - 1, sp, par] = f[sp][par]
            x1[p, sp, par] = (x0[p, sp, par] + HALF * f[sp][par]) * m

        @pl.when(p == 1)
        def _():
            start(p_v1, o_v1, p_kc, o_kc)

    loop(1, 4, body_a1)

    def body_a2(p):
        @pl.when(p == 1)
        def _():
            arrived(p_v1)

        @pl.when(p == 3)
        def _():
            arrived(o_v1)

        g = fine_rate(x1, kn, p)
        m = masked(p)
        for sp, par in each():
            r, f = g[sp][par], f0[p - 1, sp, par]
            x2[p, sp, par] = (x1[p, sp, par] + HALF * r) * m
            tq0[p - 1, sp, par] = S0[0] * f + S0[1] * r
            tq1[p - 1, sp, par] = S1[0] * f + S1[1] * r

        @pl.when(p == 1)
        def _():
            start(p_v2, o_v2)

    loop(1, 4, body_a2)

    def add_last(buf, p):
        g = fine_rate(buf, kn, p)
        for sp, par in each():
            tq0[p - 1, sp, par] = tq0[p - 1, sp, par] + S0[2] * g[sp][par]
            tq1[p - 1, sp, par] = tq1[p - 1, sp, par] + S1[2] * g[sp][par]

    def body_a3(i):
        p = 2 - i

        @pl.when(p == 1)
        def _():
            arrived(p_v2)

        add_last(x2, p)

    loop(0, 2, body_a3)

    w0, w1, w2 = (restrict(x, 1, 2) for x in (x0, x1, x2))
    q0, q1 = restrict(tq0, 0, 1), restrict(tq1, 0, 1)
    c1 = w0 + q0
    d1c[2] = c1 - w1
    b2c[1] = c1 + q1 + HALF * (local_rate(c1) - local_rate(w1))
    wpk[0] = w0
    wpk[1] = w2

    def spread(buf, at, cond):
        return [
            copy(buf.at[at], buf.at[3], t, outer, both(cond, has_out)),
            copy(buf.at[at], buf.at[4], t, far_in, both(cond, has_far), both(cond, has_out)),
            copy(buf.at[at], buf.at[0], t, far_out, both(cond, has_out), both(cond, has_far)),
            copy(buf.at[at], buf.at[1], t, partner, cond),
        ]

    def beside(buf, cond):
        return [
            copy(buf.at[1], buf.at[2], t, outer, both(cond, has_out)),
            copy(buf.at[1], buf.at[0], t, partner, cond),
        ]

    r2 = spread(d1c, 2, always) + beside(b2c, always) + [copy(wpk, wi, t, partner, always)]
    start(*r2)
    w0o = restrict(x0, 3, 4)
    arrived(p_kc, o_kc, o_v2)
    w2o = restrict(x2, 3, 4)
    arrived(*r2)
    w0s = (wi[0], w0, w0o)
    w2s = (wi[1], w2, w2o)

    def corrected(d, b, j):
        r = b[j] + kc[j] * coarse_lap(d[j], d[j + 1], d[j + 2])
        return r * m_out if j == 2 else r

    c02 = [corrected(d1c, b2c, j) for j in range(3)]
    for j in range(3):
        ddy[j] = c02[j] - w2s[j]

    @pl.when(first)
    def _():
        for j in range(3):
            dd1[j] = d1c[j + 1]
            dd2[j] = ddy[j]

    r3 = spread(d11c, 2, second) + beside(b11c, second)

    @pl.when(second)
    def _():
        d10 = [c02[j] - w0s[j] for j in range(3)]
        for j in range(3):
            dd0[j] = d10[j]
        c11 = c02[1] + q0 + kc[1] * coarse_lap(*d10) + HALF * (local_rate(c02[1]) - local_rate(w0))
        d11c[2] = c11 - w1
        b11c[1] = c11 + q1 + HALF * (local_rate(c11) - local_rate(w1))

    start(*r3)
    arrived(*r3)

    @pl.when(second)
    def _():
        for j in range(3):
            dd1[j] = d11c[j + 1]
            dd2[j] = corrected(d11c, b11c, j) - w2s[j]

    def add_prolonged(dst, src, dd, p):
        j = (p + 1) // 2
        up = prolong(dd[j])
        for sp, par in each():
            dst[p, sp, par] = src[p, sp, par] + up[sp]

    def body_u(p):
        add_prolonged(u1, x1, dd1, p)
        add_prolonged(u2, x2, dd2, p)

    loop(0, 5, body_u)

    @pl.when(first)
    def _():
        def body(p):
            for sp, par in each():
                g0[p - 1, sp, par] = f0[p - 1, sp, par]
                base[p - 1, sp, par] = x0[p, sp, par]
        loop(1, 4, body)

    @pl.when(second)
    def _():
        def body_uy(p):
            add_prolonged(u0, x0, dd0, p)
            add_prolonged(y, x2, ddy, p)
        loop(0, 5, body_uy)

        def body(p):
            f = fine_rate(u0, kn, p)
            r = fine_rate(y, kn, p)
            for sp, par in each():
                f0[p - 1, sp, par] = f[sp][par]
                g0[p - 1, sp, par] = r[sp][par]
                base[p - 1, sp, par] = y[p, sp, par] + HALF * (r[sp][par] - f[sp][par])
        loop(1, 4, body)

    p_v1p = copy(v1p.at[1], v1p.at[0], t, partner, always)
    p_v2p = copy(v2p.at[1], v2p.at[0], t, partner, always)
    o_v2p = copy(v2p.at[2], v2p.at[3], t, outer, has_out)

    def body_c1(p):
        fa = fine_rate(u1, kn, p)
        fb = fine_rate(u2, kn, p)
        m = masked(p)
        for sp, par in each():
            f, a, b = f0[p - 1, sp, par], fa[sp][par], fb[sp][par]
            v1p[p, sp, par] = (base[p - 1, sp, par] + S0[0] * f + S0[1] * a + S0[2] * b) * m
            ex[p - 1, sp, par] = S1[0] * f + (S1[1] - HALF) * a + S1[2] * b

        @pl.when(p == 1)
        def _():
            start(p_v1p)

    loop(1, 4, body_c1)

    def body_c2(i):
        p = 2 - i

        @pl.when(p == 1)
        def _():
            arrived(p_v1p)

        g = fine_rate(v1p, kn, p)
        for sp, par in each():
            r, z = g[sp][par], g0[p - 1, sp, par]
            v2p[p, sp, par] = v1p[p, sp, par] + ex[p - 1, sp, par] + HALF * r
            tq0[p - 1, sp, par] = S0[0] * z + S0[1] * r
            tq1[p - 1, sp, par] = S1[0] * z + S1[1] * r

        @pl.when(p == 2)
        def _():
            start(o_v2p)

        @pl.when(p == 1)
        def _():
            start(p_v2p)

    loop(0, 2, body_c2)

    def body_c3(p):
        @pl.when(p == 1)
        def _():
            arrived(p_v2p)

        @pl.when(p == 2)
        def _():
            arrived(o_v2p)

        add_last(v2p, p)

    loop(1, 3, body_c3)

    w1, w2 = restrict(v1p, 1, 2), restrict(v2p, 1, 2)
    q0, q1 = restrict(tq0, 0, 1), restrict(tq1, 0, 1)

    r5 = beside(d5, first)
    r6 = [copy(c5own.at[0], c5.at[at], 1, s, both(first, cond), both(second, back))
          for at, cond, back, s in ((3, has_out, has_out, outer), (4, has_far, has_out, far_in),
                                    (0, has_out, has_far, far_out), (2, always, always, me),
                                    (1, always, always, partner))]
    r7 = spread(w0p, 2, second) + beside(a1p, second) + beside(w1p, second)

    @pl.when(first)
    def _():
        c1 = w0 + q0
        d5[1] = c1 - w1
        start(*r5)
        b = c1 + q1 + HALF * (local_rate(c1) - local_rate(w1))
        arrived(*r5)
        end = b + kc[1] * coarse_lap(d5[0], d5[1], d5[2])
        c5own[0] = end
        start(*r6)
        dd2[1] = end - w2

    @pl.when(second)
    def _():
        w0n = restrict(y, 1, 2)
        w0p[2] = w0n
        a1p[1] = q0 - HALF * local_rate(w0n)
        w1p[1] = w1
        start(*r7)
        arrived(*r7)

    arrived(*r6)

    @pl.when(second)
    def _():
        d10 = [c5[j] - w0p[j] for j in range(5)]
        c11 = []
        for j in range(3):
            r = c5[j + 1] + a1p[j] + kc[j] * coarse_lap(d10[j], d10[j + 1], d10[j + 2]) + HALF * local_rate(c5[j + 1])
            c11.append(r * m_out if j == 2 else r)
        d11 = [c11[j] - w1p[j] for j in range(3)]
        end = c11[1] + q1 + kc[1] * coarse_lap(*d11) + HALF * (local_rate(c11[1]) - local_rate(w1))
        dd2[1] = end - w2

    up = prolong(dd2[1])
    for p, plane in ((1, 1 - c), (2, c)):
        for sp, par in each():
            out_ref[0, sp, plane, pl.ds(par, 64, stride=2), :] = v2p[p, sp, par] + up[sp]

    for cond, cp in copies:
        when(cond, cp.wait_send)


def shards(n, initial, kappa):
    fine = lambda k: pltpu.VMEM((k, 2, 2, 64, 128), F32)
    coarse = lambda k: pltpu.VMEM((k, 64, 128), F32)
    return pl.pallas_call(
        functools.partial(kernel, n),
        out_shape=jax.ShapeDtypeStruct((1,) + initial.shape, F32),
        in_specs=[pl.BlockSpec(memory_space=pl.ANY)] * 2,
        out_specs=pl.BlockSpec(memory_space=pltpu.VMEM),
        scratch_shapes=[
            pltpu.VMEM((5, 2, 128, 128), F32), pltpu.VMEM((3, 128, 128), F32),
            fine(5), fine(5), fine(5), fine(3), fine(3), fine(3), fine(5), fine(5), fine(5), fine(5), fine(3), fine(3),
            fine(3), fine(4), fine(4),
            coarse(5), coarse(3), coarse(3), coarse(2), coarse(2), coarse(5), coarse(3), coarse(3), coarse(3), coarse(3),
            coarse(3), coarse(3), coarse(5), coarse(1), coarse(5), coarse(3), coarse(3),
            pltpu.SemaphoreType.DMA((4,)), pltpu.SemaphoreType.DMA((N_COPIES,)), pltpu.SemaphoreType.DMA((N_COPIES,)),
        ],
        compiler_params=pltpu.CompilerParams(
            collective_id=0, has_side_effects=True, vmem_limit_bytes=40 * 1024 * 1024),
    )(initial, kappa)


def solution(mesh):
    return jax.shard_map(
        functools.partial(shards, mesh.shape["space"]),
        mesh=mesh,
        in_specs=(P(None, "space", None, None), P("space", None, None)),
        out_specs=P("tm", None, "space", None, None),
        check_vma=False,
    )
```

time: 514 us -> 52.9 us (0.10); the launches traced: 504 us -> 52.8 us
  local copies, waits for them, and re-layouts: 252 us -> 2.56 us
  starting transfers between devices: 165 us -> 0 us
  Pallas kernels: 0 us -> 50.2 us
  other arithmetic: 44.1 us -> 0 us
  waiting for transfers between devices: 41.5 us -> 0 us
    another operation x24 -> x0, local copies, waits for them, and re-layouts: 183 us -> none  [react(): return jnp.stack([rate_a, rate_b], axis=-4)]
    ppermute x35 -> x0, starting transfers between devices: 165 us -> none  [the longest x16 106 us: padded_2(): lax.ppermute(lax.slice_in_dim(block, 0, width, axis=dim), axis, backward)]
    reduce_sum x7 -> x0, local copies, waits for them, and re-layouts: 64.1 us -> none  [restrict(): return 0.125 * jnp.sum(blocks, axis=(-5, -3, -1))]
    pallas_call x0 -> x1, Pallas kernels: none -> 50.2 us  [shards(): pl.pallas_call(functools.partial(kernel, n), out_shape=jax.ShapeDtypeStru...]
    ppermute x35 -> x0, waiting for transfers between devices: 41.5 us -> none  [the longest x16 24.8 us: padded_2(): lax.ppermute(lax.slice_in_dim(block, block.shape[dim] - width, None, axis...]
    reduce_sum x14 -> x0, other arithmetic: 31.1 us -> none  [restrict(): return 0.125 * jnp.sum(blocks, axis=(-5, -3, -1))]
    concatenate x16 -> x0, other arithmetic: 6.23 us -> none  [padded_2(): block = jnp.concatenate([low, block, high], axis=dim)]
  transfers between devices with their start and end apart: 35 -> 0, of which waited for: 11 -> 0; matrix products, arithmetic and copies ran while one was open for 33% -> 0% of each run, Pallas kernels for 0% -> 0%
where the time goes in v1:
time: 52.9 us; the launch traced here: 52.8 us
  Pallas kernels  50.2 us (95%)
  local copies, waits for them, and re-layouts  2.56 us (5%)
    pallas_call x1, Pallas kernels, shards(): pl.pallas_call(functools.partial(kernel, n), out_shape=jax.ShapeDtypeStru...  50.2 us
    unnamed x5, local copies, waits for them, and re-layouts  2.56 us

profile of v1, /device:TPU:27, one launch (start us, length us, event | category | flops | bytes accessed | tf_op | source)
XLA Modules:
  0.0 52.8 jit_solution(11629854995201521867)
XLA Ops:
  0.0 0.0 copy-start
  0.0 0.9 %copy-done = f32[2,2,128,128]{3,2,1,0:T(8,128)S(1)} copy-done((f32[2,2,128,128]{3,2,1,0:T(8,128)S(1)}, f32[2,2,128,128]{3,2,1,0:T(8,128)}, u32[]{:S(2)}) %copy-start) | copy-done | bytes 262168
  1.0 0.0 copy-start.1
  1.0 0.9 %copy-done.1 = f32[2,128,128]{2,1,0:T(8,128)S(1)} copy-done((f32[2,128,128]{2,1,0:T(8,128)S(1)}, f32[2,128,128]{2,1,0:T(8,128)}, u32[]{:S(2)}) %copy-start.1) | copy-done | bytes 131096
  1.9 50.2 %shard_map.28 = f32[1,2,2,128,128]{4,3,2,1,0:T(8,128)S(1)} custom-call(f32[2,2,128,128]{3,2,1,0:T(8,128)S(1)} %copy-done, f32[2,128,128]{2,1,0:T(8,128)S(1)} %copy-done.1), custom_call_target="tpu_custom_call" | custom-call | tf_op jit(solution)/shard_map/pallas_call | solution.py:487
  52.1 0.7 %copy.4 = f32[1,2,2,128,128]{4,3,2,1,0:T(8,128)} copy(f32[1,2,2,128,128]{4,3,2,1,0:T(8,128)S(1)} %shard_map.28) | data formatting | bytes 524288
Async XLA Ops:
  0.0 0.9 %copy-start = (f32[2,2,128,128]{3,2,1,0:T(8,128)S(1)}, f32[2,2,128,128]{3,2,1,0:T(8,128)}, u32[]{:S(2)}) copy-start(f32[2,2,128,128]{3,2,1,0:T(8,128)} %init_ref.1) | copy-start | bytes 786436
  1.0 0.9 %copy-start.1 = (f32[2,128,128]{2,1,0:T(8,128)S(1)}, f32[2,128,128]{2,1,0:T(8,128)}, u32[]{:S(2)}) copy-start(f32[2,128,128]{2,1,0:T(8,128)} %kap_ref.1) | copy-start | bytes 393220

commit v2 on v1

--- a/solution.py
+++ b/solution.py
@@ -91,7 +91,7 @@
 def kernel(
     n, init_ref, kap_ref, out_ref,
     nat, kn, x0, x1, x2, f0, tq0, tq1, u0, u1, u2, y, base, g0, ex, v1p, v2p,
-    d1c, b2c, kc, wi, wpk, d11c, b11c, dd0, dd1, dd2, ddy, d5, c5, c5own, w0p, a1p, w1p,
+    d1c, b2c, kc, wi, wpk, d11c, b11c, dd0, dd1, dd2, ddy, d5, c5, c5own, w0p, a1p, w1p, e3,
     lsem, ssem, rsem,
 ):
     me = lax.axis_index("space")
@@ -156,7 +156,6 @@
         zero_plane = jnp.zeros((2, 2, 64, 128), F32)
         for buf in (x1, x2):
             buf[4] = zero_plane
-        v2p[3] = zero_plane
         nat[3] = jnp.zeros((2, 128, 128), F32)
         nat[4] = jnp.zeros((2, 128, 128), F32)
         kn[2] = jnp.zeros((128, 128), F32)
@@ -166,27 +165,30 @@
             buf[4] = zero
         for buf in (b2c, kc, b11c, d5, a1p, w1p):
             buf[2] = zero
+        e3[1] = zero
 
     @pl.when(jnp.logical_not(has_far))
     def _():
         zero = jnp.zeros((64, 128), F32)
         for buf in (d1c, d11c, c5, w0p):
             buf[0] = zero
-
+        e3[0] = zero
+
+    v2p[3] = jnp.zeros((2, 2, 64, 128), F32)
     pl.semaphore_wait(barrier, 3 + 4 * has_out.astype(jnp.int32) + 2 * has_far.astype(jnp.int32))
-
-    p_init = copy(init_ref.at[:, 1 - c], nat.at[0], t, partner, always)
-    o_init = copy(init_ref.at[:, c], nat.at[3], t, outer, has_out)
-    o_kap = copy(kap_ref.at[c], kn.at[2], t, outer, has_out)
-    o_init2 = copy(init_ref.at[:, 1 - c], nat.at[4], t, outer, has_out)
-    start(p_init, o_init, o_kap, o_init2)
-
-    def convert(p):
-        for sp, par in each():
-            x0[p, sp, par] = nat[p, sp, pl.ds(par, 64, stride=2), :]
 
     for cp in locals_:
         cp.wait()
+    p_init = copy(nat.at[1], nat.at[0], t, partner, always)
+    o_init = copy(nat.at[2], nat.at[3], t, outer, has_out)
+    o_kap = copy(kn.at[1], kn.at[2], t, outer, has_out)
+    o_init2 = copy(nat.at[1], nat.at[4], t, outer, has_out)
+    start(p_init, o_init, o_kap, o_init2)
+
+    def convert(p):
+        for sp, par in each():
+            x0[p, sp, par] = nat[p, sp, pl.ds(par, 64, stride=2), :]
+
     convert(1)
     convert(2)
     ks = (kn[0, pl.ds(0, 64, stride=2), :] + kn[0, pl.ds(1, 64, stride=2), :]
@@ -328,13 +330,6 @@
         b11c[1] = c11 + q1 + HALF * (local_rate(c11) - local_rate(w1))
 
     start(*r3)
-    arrived(*r3)
-
-    @pl.when(second)
-    def _():
-        for j in range(3):
-            dd1[j] = d11c[j + 1]
-            dd2[j] = corrected(d11c, b11c, j) - w2s[j]
 
     def add_prolonged(dst, src, dd, p):
         j = (p + 1) // 2
@@ -342,11 +337,7 @@
         for sp, par in each():
             dst[p, sp, par] = src[p, sp, par] + up[sp]
 
-    def body_u(p):
-        add_prolonged(u1, x1, dd1, p)
-        add_prolonged(u2, x2, dd2, p)
-
-    loop(0, 5, body_u)
+    r7a = spread(w0p, 2, second)
 
     @pl.when(first)
     def _():
@@ -362,6 +353,8 @@
             add_prolonged(u0, x0, dd0, p)
             add_prolonged(y, x2, ddy, p)
         loop(0, 5, body_uy)
+        w0p[2] = restrict(y, 1, 2)
+        start(*r7a)
 
         def body(p):
             f = fine_rate(u0, kn, p)
@@ -372,9 +365,23 @@
                 base[p - 1, sp, par] = y[p, sp, par] + HALF * (r[sp][par] - f[sp][par])
         loop(1, 4, body)
 
+    arrived(*r3)
+
+    @pl.when(second)
+    def _():
+        for j in range(3):
+            dd1[j] = d11c[j + 1]
+            dd2[j] = corrected(d11c, b11c, j) - w2s[j]
+
+    def body_u(p):
+        add_prolonged(u1, x1, dd1, p)
+        add_prolonged(u2, x2, dd2, p)
+
+    loop(0, 5, body_u)
+
     p_v1p = copy(v1p.at[1], v1p.at[0], t, partner, always)
     p_v2p = copy(v2p.at[1], v2p.at[0], t, partner, always)
-    o_v2p = copy(v2p.at[2], v2p.at[3], t, outer, has_out)
+    r_e = [copy(e3.at[2], e3.at[1], t, outer, has_out), copy(e3.at[2], e3.at[0], t, far_out, has_out, has_far)]
 
     def body_c1(p):
         fa = fine_rate(u1, kn, p)
@@ -407,7 +414,11 @@
 
         @pl.when(p == 2)
         def _():
-            start(o_v2p)
+            k = [kn[2, pl.ds(par, 64, stride=2), :] for par in range(2)]
+            su = k[0] * v2p[2, 0, 0] + k[1] * v2p[2, 0, 1]
+            sv = k[0] * v2p[2, 1, 0] + k[1] * v2p[2, 1, 1]
+            e3[2] = 0.125 * pairs(su, 0.5 * sv)
+            start(*r_e)
 
         @pl.when(p == 1)
         def _():
@@ -415,18 +426,16 @@
 
     loop(0, 2, body_c2)
 
-    def body_c3(p):
+    def body_c3(i):
+        p = 2 - i
+
         @pl.when(p == 1)
         def _():
             arrived(p_v2p)
 
-        @pl.when(p == 2)
-        def _():
-            arrived(o_v2p)
-
         add_last(v2p, p)
 
-    loop(1, 3, body_c3)
+    loop(0, 2, body_c3)
 
     w1, w2 = restrict(v1p, 1, 2), restrict(v2p, 1, 2)
     q0, q1 = restrict(tq0, 0, 1), restrict(tq1, 0, 1)
@@ -436,28 +445,36 @@
           for at, cond, back, s in ((3, has_out, has_out, outer), (4, has_far, has_out, far_in),
                                     (0, has_out, has_far, far_out), (2, always, always, me),
                                     (1, always, always, partner))]
-    r7 = spread(w0p, 2, second) + beside(a1p, second) + beside(w1p, second)
+    r7 = beside(a1p, second) + beside(w1p, second)
 
     @pl.when(first)
     def _():
+        d5[1] = w0 + q0 - w1
+        start(*r5)
+
+    @pl.when(second)
+    def _():
+        w1p[1] = w1
+        a1p[1] = q0 - HALF * local_rate(w0p[2])
+        start(*r7)
+
+    arrived(*r_e)
+    e_own = (S0[2] * e3[0], S0[2] * e3[1], S0[2] * e3[2])
+    q0 = q0 + e_own[1]
+    q1 = q1 + S1[2] * e3[1]
+
+    @pl.when(first)
+    def _():
         c1 = w0 + q0
-        d5[1] = c1 - w1
-        start(*r5)
         b = c1 + q1 + HALF * (local_rate(c1) - local_rate(w1))
         arrived(*r5)
-        end = b + kc[1] * coarse_lap(d5[0], d5[1], d5[2])
+        end = b + kc[1] * coarse_lap(d5[0] + e_own[0], c1 - w1, d5[2] + e_own[2])
         c5own[0] = end
         start(*r6)
         dd2[1] = end - w2
 
-    @pl.when(second)
-    def _():
-        w0n = restrict(y, 1, 2)
-        w0p[2] = w0n
-        a1p[1] = q0 - HALF * local_rate(w0n)
-        w1p[1] = w1
-        start(*r7)
-        arrived(*r7)
+    arrived(*r7a)
+    arrived(*r7)
 
     arrived(*r6)
 
@@ -466,7 +483,7 @@
         d10 = [c5[j] - w0p[j] for j in range(5)]
         c11 = []
         for j in range(3):
-            r = c5[j + 1] + a1p[j] + kc[j] * coarse_lap(d10[j], d10[j + 1], d10[j + 2]) + HALF * local_rate(c5[j + 1])
+            r = c5[j + 1] + (a1p[j] + e_own[j]) + kc[j] * coarse_lap(d10[j], d10[j + 1], d10[j + 2]) + HALF * local_rate(c5[j + 1])
             c11.append(r * m_out if j == 2 else r)
         d11 = [c11[j] - w1p[j] for j in range(3)]
         end = c11[1] + q1 + kc[1] * coarse_lap(*d11) + HALF * (local_rate(c11[1]) - local_rate(w1))
@@ -487,18 +504,18 @@
     return pl.pallas_call(
         functools.partial(kernel, n),
         out_shape=jax.ShapeDtypeStruct((1,) + initial.shape, F32),
-        in_specs=[pl.BlockSpec(memory_space=pl.ANY)] * 2,
+        in_specs=[pl.BlockSpec(memory_space=pltpu.HBM)] * 2,
         out_specs=pl.BlockSpec(memory_space=pltpu.VMEM),
         scratch_shapes=[
             pltpu.VMEM((5, 2, 128, 128), F32), pltpu.VMEM((3, 128, 128), F32),
             fine(5), fine(5), fine(5), fine(3), fine(3), fine(3), fine(5), fine(5), fine(5), fine(5), fine(3), fine(3),
             fine(3), fine(4), fine(4),
             coarse(5), coarse(3), coarse(3), coarse(2), coarse(2), coarse(5), coarse(3), coarse(3), coarse(3), coarse(3),
-            coarse(3), coarse(3), coarse(5), coarse(1), coarse(5), coarse(3), coarse(3),
+            coarse(3), coarse(3), coarse(5), coarse(1), coarse(5), coarse(3), coarse(3), coarse(3),
             pltpu.SemaphoreType.DMA((4,)), pltpu.SemaphoreType.DMA((N_COPIES,)), pltpu.SemaphoreType.DMA((N_COPIES,)),
         ],
         compiler_params=pltpu.CompilerParams(
-            collective_id=0, has_side_effects=True, vmem_limit_bytes=40 * 1024 * 1024),
+            collective_id=0, has_side_effects=True, vmem_limit_bytes=63 * 1024 * 1024),
     )(initial, kappa)
 
 

time: 52.9 us -> 47.1 us (0.89)
  the two profiles are of different devices: /device:TPU:27 before, /device:TPU:26 now
where the time goes in v2:
time: 47.1 us; the launch traced here: 47 us
  Pallas kernels  45.3 us (96%)
  local copies, waits for them, and re-layouts  1.67 us (4%)
    pallas_call x1, Pallas kernels, shards(): pl.pallas_call(functools.partial(kernel, n), out_shape=jax.ShapeDtypeStru...  45.3 us
    unnamed x1, local copies, waits for them, and re-layouts  1.67 us

profile of v2, /device:TPU:26, one launch (start us, length us, event | category | flops | bytes accessed | tf_op | source)
XLA Modules:
  0.0 47.0 jit_solution(1194409374646948675)
XLA Ops:
  0.0 45.3 %shard_map.28 = f32[1,2,2,128,128]{4,3,2,1,0:T(8,128)} custom-call(f32[2,2,128,128]{3,2,1,0:T(8,128)} %init_ref.1, f32[2,128,128]{2,1,0:T(8,128)} %kap_ref.1), custom_call_target="tpu_custom_call" | custom-call | tf_op jit(solution)/shard_map/pallas_call | solution.py:504
  45.3 1.7 %copy.4 = f32[1,2,2,128,128]{4,3,2,1,0:T(8,128)} copy(f32[1,2,2,128,128]{4,3,2,1,0:T(8,128)} %shard_map.28) | data formatting | bytes 524288

commit v3 on v2

--- a/solution.py
+++ b/solution.py
@@ -90,8 +90,8 @@
 
 def kernel(
     n, init_ref, kap_ref, out_ref,
-    nat, kn, x0, x1, x2, f0, tq0, tq1, u0, u1, u2, y, base, g0, ex, v1p, v2p,
-    d1c, b2c, kc, wi, wpk, d11c, b11c, dd0, dd1, dd2, ddy, d5, c5, c5own, w0p, a1p, w1p, e3,
+    nat, kn, x0, x1, x2, f0, g1, g2, g0, base, ex, v1p, v2p,
+    d1c, b2c, kc, wi, wpk, d11c, b11c, dd, pd, td, d5, c5, c5own, a1p, e3,
     lsem, ssem, rsem,
 ):
     me = lax.axis_index("space")
@@ -105,6 +105,12 @@
     has_far = jnp.logical_and(far_in >= 0, far_in < n)
     always = None
     first, second = t == 0, t == 1
+    def across(other):
+        row = jnp.logical_and(other // 2 != me // 2, other // 4 == me // 4)
+        return jnp.where(row, 1 - t, t)
+
+    t_out, t_fin, t_fout = across(outer), across(far_in), across(far_out)
+
     m_out = jnp.where(has_out, 1.0, 0.0).astype(F32)
 
     def when(cond, fn):
@@ -160,17 +166,17 @@
         nat[4] = jnp.zeros((2, 128, 128), F32)
         kn[2] = jnp.zeros((128, 128), F32)
         zero = jnp.zeros((64, 128), F32)
-        for buf in (d1c, d11c, c5, w0p):
+        for buf in (d1c, d11c, c5):
             buf[3] = zero
             buf[4] = zero
-        for buf in (b2c, kc, b11c, d5, a1p, w1p):
+        for buf in (b2c, kc, b11c, d5, a1p):
             buf[2] = zero
         e3[1] = zero
 
     @pl.when(jnp.logical_not(has_far))
     def _():
         zero = jnp.zeros((64, 128), F32)
-        for buf in (d1c, d11c, c5, w0p):
+        for buf in (d1c, d11c, c5):
             buf[0] = zero
         e3[0] = zero
 
@@ -180,9 +186,9 @@
     for cp in locals_:
         cp.wait()
     p_init = copy(nat.at[1], nat.at[0], t, partner, always)
-    o_init = copy(nat.at[2], nat.at[3], t, outer, has_out)
-    o_kap = copy(kn.at[1], kn.at[2], t, outer, has_out)
-    o_init2 = copy(nat.at[1], nat.at[4], t, outer, has_out)
+    o_init = copy(nat.at[2], nat.at[3], t_out, outer, has_out)
+    o_kap = copy(kn.at[1], kn.at[2], t_out, outer, has_out)
+    o_init2 = copy(nat.at[1], nat.at[4], t_out, outer, has_out)
     start(p_init, o_init, o_kap, o_init2)
 
     def convert(p):
@@ -195,7 +201,7 @@
           + kn[1, pl.ds(0, 64, stride=2), :] + kn[1, pl.ds(1, 64, stride=2), :])
     kc[1] = (0.125 * HALF / 4.0) * pairs(ks, 0.5 * ks)
     p_kc = copy(kc.at[1], kc.at[0], t, partner, always)
-    o_kc = copy(kc.at[1], kc.at[2], t, outer, has_out)
+    o_kc = copy(kc.at[1], kc.at[2], t_out, outer, has_out)
 
     def masked(p):
         return jnp.where(p == 3, m_out, 1.0).astype(F32)
@@ -207,9 +213,9 @@
         lax.fori_loop(lo, hi, step, 0)
 
     p_v1 = copy(x1.at[1], x1.at[0], t, partner, always)
-    o_v1 = copy(x1.at[1], x1.at[4], t, outer, has_out)
+    o_v1 = copy(x1.at[1], x1.at[4], t_out, outer, has_out)
     p_v2 = copy(x2.at[1], x2.at[0], t, partner, always)
-    o_v2 = copy(x2.at[1], x2.at[4], t, outer, has_out)
+    o_v2 = copy(x2.at[1], x2.at[4], t_out, outer, has_out)
 
     arrived(p_init)
     convert(0)
@@ -245,10 +251,8 @@
         g = fine_rate(x1, kn, p)
         m = masked(p)
         for sp, par in each():
-            r, f = g[sp][par], f0[p - 1, sp, par]
-            x2[p, sp, par] = (x1[p, sp, par] + HALF * r) * m
-            tq0[p - 1, sp, par] = S0[0] * f + S0[1] * r
-            tq1[p - 1, sp, par] = S1[0] * f + S1[1] * r
+            g1[p - 1, sp, par] = g[sp][par]
+            x2[p, sp, par] = (x1[p, sp, par] + HALF * g[sp][par]) * m
 
         @pl.when(p == 1)
         def _():
@@ -256,11 +260,10 @@
 
     loop(1, 4, body_a2)
 
-    def add_last(buf, p):
+    def store_rate(dst, buf, p):
         g = fine_rate(buf, kn, p)
         for sp, par in each():
-            tq0[p - 1, sp, par] = tq0[p - 1, sp, par] + S0[2] * g[sp][par]
-            tq1[p - 1, sp, par] = tq1[p - 1, sp, par] + S1[2] * g[sp][par]
+            dst[p - 1, sp, par] = g[sp][par]
 
     def body_a3(i):
         p = 2 - i
@@ -269,38 +272,55 @@
         def _():
             arrived(p_v2)
 
-        add_last(x2, p)
+        store_rate(g2, x2, p)
 
     loop(0, 2, body_a3)
 
     w0, w1, w2 = (restrict(x, 1, 2) for x in (x0, x1, x2))
-    q0, q1 = restrict(tq0, 0, 1), restrict(tq1, 0, 1)
+    rf, r1, r2 = (restrict(x, 0, 1) for x in (f0, g1, g2))
+    q0 = S0[0] * rf + S0[1] * r1 + S0[2] * r2
+    q1 = S1[0] * rf + S1[1] * r1 + S1[2] * r2
     c1 = w0 + q0
     d1c[2] = c1 - w1
     b2c[1] = c1 + q1 + HALF * (local_rate(c1) - local_rate(w1))
     wpk[0] = w0
     wpk[1] = w2
 
-    def spread(buf, at, cond):
+    def spread(buf, at, cond, t_out=t, t_fin=t, t_fout=t):
         return [
-            copy(buf.at[at], buf.at[3], t, outer, both(cond, has_out)),
-            copy(buf.at[at], buf.at[4], t, far_in, both(cond, has_far), both(cond, has_out)),
-            copy(buf.at[at], buf.at[0], t, far_out, both(cond, has_out), both(cond, has_far)),
+            copy(buf.at[at], buf.at[3], t_out, outer, both(cond, has_out)),
+            copy(buf.at[at], buf.at[4], t_fin, far_in, both(cond, has_far), both(cond, has_out)),
+            copy(buf.at[at], buf.at[0], t_fout, far_out, both(cond, has_out), both(cond, has_far)),
             copy(buf.at[at], buf.at[1], t, partner, cond),
         ]
 
-    def beside(buf, cond):
+    def beside(buf, cond, t_out=t):
         return [
-            copy(buf.at[1], buf.at[2], t, outer, both(cond, has_out)),
+            copy(buf.at[1], buf.at[2], t_out, outer, both(cond, has_out)),
             copy(buf.at[1], buf.at[0], t, partner, cond),
         ]
 
-    r2 = spread(d1c, 2, always) + beside(b2c, always) + [copy(wpk, wi, t, partner, always)]
-    start(*r2)
+    round2 = spread(d1c, 2, always, t_out, t_fin, t_fout) + beside(b2c, always, t_out) + [copy(wpk, wi, t, partner, always)]
+    start(*round2)
     w0o = restrict(x0, 3, 4)
     arrived(p_kc, o_kc, o_v2)
     w2o = restrict(x2, 3, 4)
-    arrived(*r2)
+    store_rate(g2, x2, 3)
+
+    def collect(p, start_at, f):
+        for sp, par in each():
+            a, b = g1[p - 1, sp, par], g2[p - 1, sp, par]
+            base[p - 1, sp, par] = start_at[sp][par] + S0[0] * f[sp][par] + S0[1] * a + S0[2] * b
+            ex[p - 1, sp, par] = S1[0] * f[sp][par] + (S1[1] - HALF) * a + S1[2] * b
+
+    def fields(buf, p):
+        return [[buf[p, sp, par] for par in range(2)] for sp in range(2)]
+
+    def body_b1(p):
+        collect(p, fields(x0, p), fields(f0, p - 1))
+
+    loop(1, 4, body_b1)
+    arrived(*round2)
     w0s = (wi[0], w0, w0o)
     w2s = (wi[1], w2, w2o)
 
@@ -309,88 +329,92 @@
         return r * m_out if j == 2 else r
 
     c02 = [corrected(d1c, b2c, j) for j in range(3)]
-    for j in range(3):
-        ddy[j] = c02[j] - w2s[j]
+
+    def correction(i, d):
+        even = even_lane()
+        for j in range(3):
+            for sp, x in enumerate(prolong(d[j])):
+                pd[i, j, sp] = x
+                if j == 0:
+                    continue
+                low = jnp.where(iota(1) == 0, 0.0, pltpu.roll(x, 1, 1))
+                high = jnp.where(iota(1) == 127, 0.0, pltpu.roll(x, 127, 1))
+                t_ = jnp.where(even, low, high) - 3.0 * x
+                td[i, j - 1, sp, 0] = t_ + row_above(x)
+                td[i, j - 1, sp, 1] = t_ + row_below(x)
+
+    def corrected_rate(i, src, p):
+        own, across = p // 3 + 1, (2 * p - 2) % 3
+        pu, pv = pd[i, own, 0], pd[i, own, 1]
+        au, av = pd[i, across, 0], pd[i, across, 1]
+        out = [[None, None], [None, None]]
+        for par in range(2):
+            k = kn[p - 1, pl.ds(par, 64, stride=2), :]
+            u, v = src[p, 0, par], src[p, 1, par]
+            un, vn = u + pu, v + pv
+            r = un * vn * vn - u * v * v
+            out[0][par] = k * (td[i, own - 1, 0, par] + au) - r - FEED * pu
+            out[1][par] = (0.5 * k) * (td[i, own - 1, 1, par] + av) + r - (FEED + KILL) * pv
+        return out
 
     @pl.when(first)
     def _():
-        for j in range(3):
-            dd1[j] = d1c[j + 1]
-            dd2[j] = ddy[j]
+        correction(0, [d1c[j + 1] for j in range(3)])
+        correction(1, [c02[j] - w2s[j] for j in range(3)])
 
     r3 = spread(d11c, 2, second) + beside(b11c, second)
 
     @pl.when(second)
     def _():
         d10 = [c02[j] - w0s[j] for j in range(3)]
-        for j in range(3):
-            dd0[j] = d10[j]
         c11 = c02[1] + q0 + kc[1] * coarse_lap(*d10) + HALF * (local_rate(c02[1]) - local_rate(w0))
         d11c[2] = c11 - w1
         b11c[1] = c11 + q1 + HALF * (local_rate(c11) - local_rate(w1))
 
     start(*r3)
 
-    def add_prolonged(dst, src, dd, p):
-        j = (p + 1) // 2
-        up = prolong(dd[j])
-        for sp, par in each():
-            dst[p, sp, par] = src[p, sp, par] + up[sp]
-
-    r7a = spread(w0p, 2, second)
+    @pl.when(second)
+    def _():
+        correction(0, [c02[j] - w0s[j] for j in range(3)])
+        correction(1, [c02[j] - w2s[j] for j in range(3)])
+
+        def body(p):
+            df = corrected_rate(0, x0, p)
+            dr = corrected_rate(1, x2, p)
+            own = p // 3 + 1
+            y, f = fields(x2, p), fields(f0, p - 1)
+            for sp, par in each():
+                r = g2[p - 1, sp, par] + dr[sp][par]
+                f[sp][par] = f[sp][par] + df[sp][par]
+                g0[p - 1, sp, par] = r
+                y[sp][par] = y[sp][par] + pd[1, own, sp] + HALF * (r - f[sp][par])
+            collect(p, y, f)
+        loop(1, 4, body)
+        dd[0] = restrict(g0, 0, 1)
 
     @pl.when(first)
     def _():
-        def body(p):
-            for sp, par in each():
-                g0[p - 1, sp, par] = f0[p - 1, sp, par]
-                base[p - 1, sp, par] = x0[p, sp, par]
-        loop(1, 4, body)
+        dd[0] = rf
+
+    arrived(*r3)
 
     @pl.when(second)
     def _():
-        def body_uy(p):
-            add_prolonged(u0, x0, dd0, p)
-            add_prolonged(y, x2, ddy, p)
-        loop(0, 5, body_uy)
-        w0p[2] = restrict(y, 1, 2)
-        start(*r7a)
-
-        def body(p):
-            f = fine_rate(u0, kn, p)
-            r = fine_rate(y, kn, p)
-            for sp, par in each():
-                f0[p - 1, sp, par] = f[sp][par]
-                g0[p - 1, sp, par] = r[sp][par]
-                base[p - 1, sp, par] = y[p, sp, par] + HALF * (r[sp][par] - f[sp][par])
-        loop(1, 4, body)
-
-    arrived(*r3)
-
-    @pl.when(second)
-    def _():
-        for j in range(3):
-            dd1[j] = d11c[j + 1]
-            dd2[j] = corrected(d11c, b11c, j) - w2s[j]
-
-    def body_u(p):
-        add_prolonged(u1, x1, dd1, p)
-        add_prolonged(u2, x2, dd2, p)
-
-    loop(0, 5, body_u)
+        correction(0, [d11c[j + 1] for j in range(3)])
+        correction(1, [corrected(d11c, b11c, j) - w2s[j] for j in range(3)])
 
     p_v1p = copy(v1p.at[1], v1p.at[0], t, partner, always)
     p_v2p = copy(v2p.at[1], v2p.at[0], t, partner, always)
     r_e = [copy(e3.at[2], e3.at[1], t, outer, has_out), copy(e3.at[2], e3.at[0], t, far_out, has_out, has_far)]
 
     def body_c1(p):
-        fa = fine_rate(u1, kn, p)
-        fb = fine_rate(u2, kn, p)
+        fa = corrected_rate(0, x1, p)
+        fb = corrected_rate(1, x2, p)
         m = masked(p)
         for sp, par in each():
-            f, a, b = f0[p - 1, sp, par], fa[sp][par], fb[sp][par]
-            v1p[p, sp, par] = (base[p - 1, sp, par] + S0[0] * f + S0[1] * a + S0[2] * b) * m
-            ex[p - 1, sp, par] = S1[0] * f + (S1[1] - HALF) * a + S1[2] * b
+            a, b = fa[sp][par], fb[sp][par]
+            v1p[p, sp, par] = (base[p - 1, sp, par] + S0[1] * a + S0[2] * b) * m
+            ex[p - 1, sp, par] = ex[p - 1, sp, par] + (S1[1] - HALF) * a + S1[2] * b
 
         @pl.when(p == 1)
         def _():
@@ -407,10 +431,8 @@
 
         g = fine_rate(v1p, kn, p)
         for sp, par in each():
-            r, z = g[sp][par], g0[p - 1, sp, par]
-            v2p[p, sp, par] = v1p[p, sp, par] + ex[p - 1, sp, par] + HALF * r
-            tq0[p - 1, sp, par] = S0[0] * z + S0[1] * r
-            tq1[p - 1, sp, par] = S1[0] * z + S1[1] * r
+            g1[p - 1, sp, par] = g[sp][par]
+            v2p[p, sp, par] = v1p[p, sp, par] + ex[p - 1, sp, par] + HALF * g[sp][par]
 
         @pl.when(p == 2)
         def _():
@@ -433,19 +455,21 @@
         def _():
             arrived(p_v2p)
 
-        add_last(v2p, p)
+        store_rate(g2, v2p, p)
 
     loop(0, 2, body_c3)
 
     w1, w2 = restrict(v1p, 1, 2), restrict(v2p, 1, 2)
-    q0, q1 = restrict(tq0, 0, 1), restrict(tq1, 0, 1)
+    rf, r1, r2 = dd[0], restrict(g1, 0, 1), restrict(g2, 0, 1)
+    q0 = S0[0] * rf + S0[1] * r1 + S0[2] * r2
+    q1 = S1[0] * rf + S1[1] * r1 + S1[2] * r2
 
     r5 = beside(d5, first)
     r6 = [copy(c5own.at[0], c5.at[at], 1, s, both(first, cond), both(second, back))
           for at, cond, back, s in ((3, has_out, has_out, outer), (4, has_far, has_out, far_in),
                                     (0, has_out, has_far, far_out), (2, always, always, me),
                                     (1, always, always, partner))]
-    r7 = beside(a1p, second) + beside(w1p, second)
+    r7 = beside(a1p, second)
 
     @pl.when(first)
     def _():
@@ -454,8 +478,7 @@
 
     @pl.when(second)
     def _():
-        w1p[1] = w1
-        a1p[1] = q0 - HALF * local_rate(w0p[2])
+        a1p[1] = q0 - HALF * local_rate(c02[1]) - w1
         start(*r7)
 
     arrived(*r_e)
@@ -469,27 +492,27 @@
         b = c1 + q1 + HALF * (local_rate(c1) - local_rate(w1))
         arrived(*r5)
         end = b + kc[1] * coarse_lap(d5[0] + e_own[0], c1 - w1, d5[2] + e_own[2])
-        c5own[0] = end
+        c5own[0] = end - c02[1]
         start(*r6)
-        dd2[1] = end - w2
-
-    arrived(*r7a)
+        dd[1] = end - w2
+
     arrived(*r7)
 
     arrived(*r6)
 
     @pl.when(second)
     def _():
-        d10 = [c5[j] - w0p[j] for j in range(5)]
-        c11 = []
+        d11, c11 = [], None
         for j in range(3):
-            r = c5[j + 1] + (a1p[j] + e_own[j]) + kc[j] * coarse_lap(d10[j], d10[j + 1], d10[j + 2]) + HALF * local_rate(c5[j + 1])
-            c11.append(r * m_out if j == 2 else r)
-        d11 = [c11[j] - w1p[j] for j in range(3)]
-        end = c11[1] + q1 + kc[1] * coarse_lap(*d11) + HALF * (local_rate(c11[1]) - local_rate(w1))
-        dd2[1] = end - w2
-
-    up = prolong(dd2[1])
+            c10 = c5[j + 1] + c02[j]
+            r = c10 + (a1p[j] + e_own[j]) + kc[j] * coarse_lap(c5[j], c5[j + 1], c5[j + 2]) + HALF * local_rate(c10)
+            if j == 1:
+                c11 = r + w1
+            d11.append(r * m_out if j == 2 else r)
+        end = c11 + q1 + kc[1] * coarse_lap(*d11) + HALF * (local_rate(c11) - local_rate(w1))
+        dd[1] = end - w2
+
+    up = prolong(dd[1])
     for p, plane in ((1, 1 - c), (2, c)):
         for sp, par in each():
             out_ref[0, sp, plane, pl.ds(par, 64, stride=2), :] = v2p[p, sp, par] + up[sp]
@@ -503,15 +526,15 @@
     coarse = lambda k: pltpu.VMEM((k, 64, 128), F32)
     return pl.pallas_call(
         functools.partial(kernel, n),
-        out_shape=jax.ShapeDtypeStruct((1,) + initial.shape, F32),
+        out_shape=pltpu.VMEM((1,) + initial.shape, F32),
         in_specs=[pl.BlockSpec(memory_space=pltpu.HBM)] * 2,
         out_specs=pl.BlockSpec(memory_space=pltpu.VMEM),
         scratch_shapes=[
             pltpu.VMEM((5, 2, 128, 128), F32), pltpu.VMEM((3, 128, 128), F32),
-            fine(5), fine(5), fine(5), fine(3), fine(3), fine(3), fine(5), fine(5), fine(5), fine(5), fine(3), fine(3),
-            fine(3), fine(4), fine(4),
-            coarse(5), coarse(3), coarse(3), coarse(2), coarse(2), coarse(5), coarse(3), coarse(3), coarse(3), coarse(3),
-            coarse(3), coarse(3), coarse(5), coarse(1), coarse(5), coarse(3), coarse(3), coarse(3),
+            fine(5), fine(5), fine(5), fine(3), fine(3), fine(3), fine(3), fine(3), fine(3), fine(4), fine(4),
+            coarse(5), coarse(3), coarse(3), coarse(2), coarse(2), coarse(5), coarse(3), coarse(2),
+            pltpu.VMEM((2, 3, 2, 64, 128), F32), pltpu.VMEM((2, 2, 2, 2, 64, 128), F32),
+            coarse(3), coarse(5), coarse(1), coarse(3), coarse(3),
             pltpu.SemaphoreType.DMA((4,)), pltpu.SemaphoreType.DMA((N_COPIES,)), pltpu.SemaphoreType.DMA((N_COPIES,)),
         ],
         compiler_params=pltpu.CompilerParams(

time: 47.1 us -> 43.2 us (0.917)
  the two profiles are of different devices: /device:TPU:26 before, /device:TPU:27 now
where the time goes in v3:
time: 43.2 us; the launch traced here: 43.1 us
  Pallas kernels  42.4 us (98%)
  local copies, waits for them, and re-layouts  0.71 us (2%)
    pallas_call x1, Pallas kernels, shards(): pl.pallas_call(functools.partial(kernel, n), out_shape=pltpu.VMEM((1,) +...  42.4 us

profile of v3, /device:TPU:27, one launch (start us, length us, event | category | flops | bytes accessed | tf_op | source)
XLA Modules:
  0.0 43.1 jit_solution(8628457821748712687)
XLA Ops:
  0.0 42.4 %shard_map.28 = f32[1,2,2,128,128]{4,3,2,1,0:T(8,128)S(1)} custom-call(f32[2,2,128,128]{3,2,1,0:T(8,128)} %init_ref.1, f32[2,128,128]{2,1,0:T(8,128)} %kap_ref.1), custom_call_target="tpu_custom_call" | custom-call | tf_op jit(solution)/shard_map/pallas_call | solution.py:527
  42.4 0.7 %copy.4 = f32[1,2,2,128,128]{4,3,2,1,0:T(8,128)} copy(f32[1,2,2,128,128]{4,3,2,1,0:T(8,128)S(1)} %shard_map.28) | data formatting | bytes 524288

commit v4 on v3

--- a/solution.py
+++ b/solution.py
@@ -41,14 +41,21 @@
     return jnp.where(iota(0) == 63, 0.0, pltpu.roll(x, 63, 0))
 
 
-def fine_rate(buf, kn, p):
+def kappas(kn, p):
+    return [kn[p, pl.ds(par, 64, stride=2), :] for par in range(2)]
+
+
+def fine_rate(buf, kn, p, below=True, above=True):
     centre = [[buf[p, sp, par] for par in range(2)] for sp in range(2)]
-    kappa = [kn[p - 1, pl.ds(par, 64, stride=2), :] for par in range(2)]
+    kappa = kappas(kn, p)
     lap = []
     for sp in range(2):
         e, o = centre[sp]
-        le = buf[p - 1, sp, 0] + buf[p + 1, sp, 0] + o + row_above(o) + beside_lanes(e, 1) - 6.0 * e
-        lo = buf[p - 1, sp, 1] + buf[p + 1, sp, 1] + e + row_below(e) + beside_lanes(o, 1) - 6.0 * o
+        le = o + row_above(o) + beside_lanes(e, 1) - 6.0 * e
+        lo = e + row_below(e) + beside_lanes(o, 1) - 6.0 * o
+        for there, q in ((below, p - 1), (above, p + 1)):
+            if there:
+                le, lo = le + buf[q, sp, 0], lo + buf[q, sp, 1]
         lap.append((le, lo))
     out = [[None, None], [None, None]]
     for par in range(2):
@@ -59,6 +66,10 @@
     return out
 
 
+def across(buf, q, kn, p):
+    return [[(k if sp == 0 else 0.5 * k) * buf[q, sp, par] for par, k in enumerate(kappas(kn, p))] for sp in range(2)]
+
+
 def each():
     return [(sp, par) for sp in range(2) for par in range(2)]
 
@@ -70,6 +81,10 @@
 def restrict(buf, a, b):
     s = [buf[a, sp, 0] + buf[a, sp, 1] + buf[b, sp, 0] + buf[b, sp, 1] for sp in range(2)]
     return 0.125 * pairs(s[0], s[1])
+
+
+def restrict_plane(g):
+    return 0.125 * pairs(g[0][0] + g[0][1], g[1][0] + g[1][1])
 
 
 def prolong(d):
@@ -105,11 +120,11 @@
     has_far = jnp.logical_and(far_in >= 0, far_in < n)
     always = None
     first, second = t == 0, t == 1
-    def across(other):
+    def other_tm(other):
         row = jnp.logical_and(other // 2 != me // 2, other // 4 == me // 4)
         return jnp.where(row, 1 - t, t)
 
-    t_out, t_fin, t_fout = across(outer), across(far_in), across(far_out)
+    t_out, t_fin, t_fout = other_tm(outer), other_tm(far_in), other_tm(far_out)
 
     m_out = jnp.where(has_out, 1.0, 0.0).astype(F32)
 
@@ -145,8 +160,8 @@
     locals_ = [
         pltpu.make_async_copy(init_ref.at[:, 1 - c], nat.at[1], lsem.at[0]),
         pltpu.make_async_copy(init_ref.at[:, c], nat.at[2], lsem.at[1]),
-        pltpu.make_async_copy(kap_ref.at[1 - c], kn.at[0], lsem.at[2]),
-        pltpu.make_async_copy(kap_ref.at[c], kn.at[1], lsem.at[3]),
+        pltpu.make_async_copy(kap_ref.at[1 - c], kn.at[1], lsem.at[2]),
+        pltpu.make_async_copy(kap_ref.at[c], kn.at[2], lsem.at[3]),
     ]
     for cp in locals_:
         cp.start()
@@ -164,7 +179,7 @@
             buf[4] = zero_plane
         nat[3] = jnp.zeros((2, 128, 128), F32)
         nat[4] = jnp.zeros((2, 128, 128), F32)
-        kn[2] = jnp.zeros((128, 128), F32)
+        kn[3] = jnp.zeros((128, 128), F32)
         zero = jnp.zeros((64, 128), F32)
         for buf in (d1c, d11c, c5):
             buf[3] = zero
@@ -180,16 +195,16 @@
             buf[0] = zero
         e3[0] = zero
 
-    v2p[3] = jnp.zeros((2, 2, 64, 128), F32)
     pl.semaphore_wait(barrier, 3 + 4 * has_out.astype(jnp.int32) + 2 * has_far.astype(jnp.int32))
 
     for cp in locals_:
         cp.wait()
     p_init = copy(nat.at[1], nat.at[0], t, partner, always)
     o_init = copy(nat.at[2], nat.at[3], t_out, outer, has_out)
-    o_kap = copy(kn.at[1], kn.at[2], t_out, outer, has_out)
+    p_kap = copy(kn.at[1], kn.at[0], t, partner, always)
+    o_kap = copy(kn.at[2], kn.at[3], t_out, outer, has_out)
     o_init2 = copy(nat.at[1], nat.at[4], t_out, outer, has_out)
-    start(p_init, o_init, o_kap, o_init2)
+    start(p_init, o_init, o_kap, o_init2, p_kap)
 
     def convert(p):
         for sp, par in each():
@@ -197,8 +212,7 @@
 
     convert(1)
     convert(2)
-    ks = (kn[0, pl.ds(0, 64, stride=2), :] + kn[0, pl.ds(1, 64, stride=2), :]
-          + kn[1, pl.ds(0, 64, stride=2), :] + kn[1, pl.ds(1, 64, stride=2), :])
+    ks = sum(kappas(kn, 1) + kappas(kn, 2))
     kc[1] = (0.125 * HALF / 4.0) * pairs(ks, 0.5 * ks)
     p_kc = copy(kc.at[1], kc.at[0], t, partner, always)
     o_kc = copy(kc.at[1], kc.at[2], t_out, outer, has_out)
@@ -235,7 +249,7 @@
 
         @pl.when(p == 1)
         def _():
-            start(p_v1, o_v1, p_kc, o_kc)
+            start(p_v1, o_v1)
 
     loop(1, 4, body_a1)
 
@@ -244,42 +258,43 @@
         def _():
             arrived(p_v1)
 
-        @pl.when(p == 3)
-        def _():
-            arrived(o_v1)
-
         g = fine_rate(x1, kn, p)
-        m = masked(p)
         for sp, par in each():
             g1[p - 1, sp, par] = g[sp][par]
-            x2[p, sp, par] = (x1[p, sp, par] + HALF * g[sp][par]) * m
+            x2[p, sp, par] = x1[p, sp, par] + HALF * g[sp][par]
 
         @pl.when(p == 1)
         def _():
-            start(p_v2, o_v2)
-
-    loop(1, 4, body_a2)
-
-    def store_rate(dst, buf, p):
-        g = fine_rate(buf, kn, p)
+            start(p_v2, p_kc, o_kc)
+
+    loop(1, 3, body_a2)
+
+    def store(dst, p, g):
         for sp, par in each():
             dst[p - 1, sp, par] = g[sp][par]
 
-    def body_a3(i):
-        p = 2 - i
-
-        @pl.when(p == 1)
-        def _():
-            arrived(p_v2)
-
-        store_rate(g2, x2, p)
-
-    loop(0, 2, body_a3)
-
+    store(g1, 3, fine_rate(x1, kn, 3, above=False))
+    store(g2, 2, fine_rate(x2, kn, 2, above=False))
     w0, w1, w2 = (restrict(x, 1, 2) for x in (x0, x1, x2))
-    rf, r1, r2 = (restrict(x, 0, 1) for x in (f0, g1, g2))
+    rf, r1 = restrict(f0, 0, 1), restrict(g1, 0, 1)
+    arrived(p_v2)
+    store(g2, 1, fine_rate(x2, kn, 1))
+    r2 = restrict(g2, 0, 1)
     q0 = S0[0] * rf + S0[1] * r1 + S0[2] * r2
     q1 = S1[0] * rf + S1[1] * r1 + S1[2] * r2
+
+    arrived(o_v1)
+    more = across(x1, 4, kn, 3)
+    for sp, par in each():
+        r = g1[2, sp, par] + more[sp][par]
+        g1[2, sp, par] = r
+        x2[3, sp, par] = (x1[3, sp, par] + HALF * r) * m_out
+    more = across(x2, 3, kn, 2)
+    for sp, par in each():
+        g2[1, sp, par] = g2[1, sp, par] + more[sp][par]
+    r2 = restrict_plane(more)
+    q0 = q0 + S0[2] * r2
+    q1 = q1 + S1[2] * r2
     c1 = w0 + q0
     d1c[2] = c1 - w1
     b2c[1] = c1 + q1 + HALF * (local_rate(c1) - local_rate(w1))
@@ -302,16 +317,15 @@
 
     round2 = spread(d1c, 2, always, t_out, t_fin, t_fout) + beside(b2c, always, t_out) + [copy(wpk, wi, t, partner, always)]
     start(*round2)
+    start(o_v2)
     w0o = restrict(x0, 3, 4)
-    arrived(p_kc, o_kc, o_v2)
-    w2o = restrict(x2, 3, 4)
-    store_rate(g2, x2, 3)
+    arrived(p_kc, o_kc)
 
     def collect(p, start_at, f):
         for sp, par in each():
             a, b = g1[p - 1, sp, par], g2[p - 1, sp, par]
-            base[p - 1, sp, par] = start_at[sp][par] + S0[0] * f[sp][par] + S0[1] * a + S0[2] * b
-            ex[p - 1, sp, par] = S1[0] * f[sp][par] + (S1[1] - HALF) * a + S1[2] * b
+            base[p, sp, par] = start_at[sp][par] + S0[0] * f[sp][par] + S0[1] * a + S0[2] * b
+            ex[p, sp, par] = S1[0] * f[sp][par] + (S1[1] - HALF) * a + S1[2] * b
 
     def fields(buf, p):
         return [[buf[p, sp, par] for par in range(2)] for sp in range(2)]
@@ -319,10 +333,15 @@
     def body_b1(p):
         collect(p, fields(x0, p), fields(f0, p - 1))
 
-    loop(1, 4, body_b1)
+    loop(1, 3, body_b1)
+    p_base = copy(base.at[1], base.at[0], t, partner, always)
+
+    @pl.when(first)
+    def _():
+        start(p_base)
+
     arrived(*round2)
     w0s = (wi[0], w0, w0o)
-    w2s = (wi[1], w2, w2o)
 
     def corrected(d, b, j):
         r = b[j] + kc[j] * coarse_lap(d[j], d[j + 1], d[j + 2])
@@ -335,32 +354,26 @@
         for j in range(3):
             for sp, x in enumerate(prolong(d[j])):
                 pd[i, j, sp] = x
-                if j == 0:
-                    continue
                 low = jnp.where(iota(1) == 0, 0.0, pltpu.roll(x, 1, 1))
                 high = jnp.where(iota(1) == 127, 0.0, pltpu.roll(x, 127, 1))
                 t_ = jnp.where(even, low, high) - 3.0 * x
-                td[i, j - 1, sp, 0] = t_ + row_above(x)
-                td[i, j - 1, sp, 1] = t_ + row_below(x)
+                td[i, j, sp, 0] = t_ + row_above(x)
+                td[i, j, sp, 1] = t_ + row_below(x)
 
     def corrected_rate(i, src, p):
-        own, across = p // 3 + 1, (2 * p - 2) % 3
+        own = (p + 1) // 2
+        beyond = own + 1 - 2 * (p % 2)
         pu, pv = pd[i, own, 0], pd[i, own, 1]
-        au, av = pd[i, across, 0], pd[i, across, 1]
+        au, av = pd[i, beyond, 0], pd[i, beyond, 1]
         out = [[None, None], [None, None]]
         for par in range(2):
-            k = kn[p - 1, pl.ds(par, 64, stride=2), :]
+            k = kappas(kn, p)[par]
             u, v = src[p, 0, par], src[p, 1, par]
             un, vn = u + pu, v + pv
             r = un * vn * vn - u * v * v
-            out[0][par] = k * (td[i, own - 1, 0, par] + au) - r - FEED * pu
-            out[1][par] = (0.5 * k) * (td[i, own - 1, 1, par] + av) + r - (FEED + KILL) * pv
+            out[0][par] = k * (td[i, own, 0, par] + au) - r - FEED * pu
+            out[1][par] = (0.5 * k) * (td[i, own, 1, par] + av) + r - (FEED + KILL) * pv
         return out
-
-    @pl.when(first)
-    def _():
-        correction(0, [d1c[j + 1] for j in range(3)])
-        correction(1, [c02[j] - w2s[j] for j in range(3)])
 
     r3 = spread(d11c, 2, second) + beside(b11c, second)
 
@@ -373,6 +386,16 @@
 
     start(*r3)
 
+    arrived(o_v2)
+    w2s = (wi[1], w2, restrict(x2, 3, 4))
+    store(g2, 3, fine_rate(x2, kn, 3))
+
+    @pl.when(first)
+    def _():
+        body_b1(3)
+        correction(0, [d1c[j + 1] for j in range(3)])
+        correction(1, [c02[j] - w2s[j] for j in range(3)])
+
     @pl.when(second)
     def _():
         correction(0, [c02[j] - w0s[j] for j in range(3)])
@@ -381,7 +404,7 @@
         def body(p):
             df = corrected_rate(0, x0, p)
             dr = corrected_rate(1, x2, p)
-            own = p // 3 + 1
+            own = (p + 1) // 2
             y, f = fields(x2, p), fields(f0, p - 1)
             for sp, par in each():
                 r = g2[p - 1, sp, par] + dr[sp][par]
@@ -390,6 +413,7 @@
                 y[sp][par] = y[sp][par] + pd[1, own, sp] + HALF * (r - f[sp][par])
             collect(p, y, f)
         loop(1, 4, body)
+        start(p_base)
         dd[0] = restrict(g0, 0, 1)
 
     @pl.when(first)
@@ -403,9 +427,16 @@
         correction(0, [d11c[j + 1] for j in range(3)])
         correction(1, [corrected(d11c, b11c, j) - w2s[j] for j in range(3)])
 
-    p_v1p = copy(v1p.at[1], v1p.at[0], t, partner, always)
     p_v2p = copy(v2p.at[1], v2p.at[0], t, partner, always)
     r_e = [copy(e3.at[2], e3.at[1], t, outer, has_out), copy(e3.at[2], e3.at[0], t, far_out, has_out, has_far)]
+
+    def second_node(p):
+        g = fine_rate(v1p, kn, p)
+        for sp, par in each():
+            g1[p - 1, sp, par] = g[sp][par]
+            v2p[p, sp, par] = v1p[p, sp, par] + ex[p, sp, par] + HALF * g[sp][par]
+
+    arrived(p_base, p_kap)
 
     def body_c1(p):
         fa = corrected_rate(0, x1, p)
@@ -413,56 +444,29 @@
         m = masked(p)
         for sp, par in each():
             a, b = fa[sp][par], fb[sp][par]
-            v1p[p, sp, par] = (base[p - 1, sp, par] + S0[1] * a + S0[2] * b) * m
-            ex[p - 1, sp, par] = ex[p - 1, sp, par] + (S1[1] - HALF) * a + S1[2] * b
-
-        @pl.when(p == 1)
-        def _():
-            start(p_v1p)
-
-    loop(1, 4, body_c1)
-
-    def body_c2(i):
-        p = 2 - i
-
-        @pl.when(p == 1)
-        def _():
-            arrived(p_v1p)
-
-        g = fine_rate(v1p, kn, p)
-        for sp, par in each():
-            g1[p - 1, sp, par] = g[sp][par]
-            v2p[p, sp, par] = v1p[p, sp, par] + ex[p - 1, sp, par] + HALF * g[sp][par]
+            v1p[p, sp, par] = (base[p, sp, par] + S0[1] * a + S0[2] * b) * m
+            ex[p, sp, par] = ex[p, sp, par] + (S1[1] - HALF) * a + S1[2] * b
 
         @pl.when(p == 2)
         def _():
-            k = [kn[2, pl.ds(par, 64, stride=2), :] for par in range(2)]
-            su = k[0] * v2p[2, 0, 0] + k[1] * v2p[2, 0, 1]
-            sv = k[0] * v2p[2, 1, 0] + k[1] * v2p[2, 1, 1]
-            e3[2] = 0.125 * pairs(su, 0.5 * sv)
-            start(*r_e)
-
-        @pl.when(p == 1)
-        def _():
+            second_node(1)
             start(p_v2p)
 
-    loop(0, 2, body_c2)
-
-    def body_c3(i):
-        p = 2 - i
-
-        @pl.when(p == 1)
-        def _():
-            arrived(p_v2p)
-
-        store_rate(g2, v2p, p)
-
-    loop(0, 2, body_c3)
+    loop(0, 4, body_c1)
+    second_node(2)
+    e3[2] = restrict_plane(across(v2p, 2, kn, 3))
+    start(*r_e)
+    store(g2, 2, fine_rate(v2p, kn, 2, above=False))
+    store(g2, 1, fine_rate(v2p, kn, 1, below=False))
 
     w1, w2 = restrict(v1p, 1, 2), restrict(v2p, 1, 2)
     rf, r1, r2 = dd[0], restrict(g1, 0, 1), restrict(g2, 0, 1)
     q0 = S0[0] * rf + S0[1] * r1 + S0[2] * r2
     q1 = S1[0] * rf + S1[1] * r1 + S1[2] * r2
+    arrived(p_v2p)
+    r2 = restrict_plane(across(v2p, 0, kn, 1))
+    q0 = q0 + S0[2] * r2
+    q1 = q1 + S1[2] * r2
 
     r5 = beside(d5, first)
     r6 = [copy(c5own.at[0], c5.at[at], 1, s, both(first, cond), both(second, back))
@@ -530,10 +534,10 @@
         in_specs=[pl.BlockSpec(memory_space=pltpu.HBM)] * 2,
         out_specs=pl.BlockSpec(memory_space=pltpu.VMEM),
         scratch_shapes=[
-            pltpu.VMEM((5, 2, 128, 128), F32), pltpu.VMEM((3, 128, 128), F32),
-            fine(5), fine(5), fine(5), fine(3), fine(3), fine(3), fine(3), fine(3), fine(3), fine(4), fine(4),
+            pltpu.VMEM((5, 2, 128, 128), F32), pltpu.VMEM((4, 128, 128), F32),
+            fine(5), fine(5), fine(5), fine(3), fine(3), fine(3), fine(3), fine(4), fine(4), fine(4), fine(3),
             coarse(5), coarse(3), coarse(3), coarse(2), coarse(2), coarse(5), coarse(3), coarse(2),
-            pltpu.VMEM((2, 3, 2, 64, 128), F32), pltpu.VMEM((2, 2, 2, 2, 64, 128), F32),
+            pltpu.VMEM((2, 3, 2, 64, 128), F32), pltpu.VMEM((2, 3, 2, 2, 64, 128), F32),
             coarse(3), coarse(5), coarse(1), coarse(3), coarse(3),
             pltpu.SemaphoreType.DMA((4,)), pltpu.SemaphoreType.DMA((N_COPIES,)), pltpu.SemaphoreType.DMA((N_COPIES,)),
         ],

time: 43.2 us -> 42.2 us (0.977)
  Pallas kernels: 42.4 us -> 41.4 us
    pallas_call x1, Pallas kernels: 42.4 us -> 41.4 us  [shards(): pl.pallas_call(functools.partial(kernel, n), out_shape=pltpu.VMEM((1,) +...]
where the time goes in v4:
time: 42.2 us; the launch traced here: 42.1 us
  Pallas kernels  41.4 us (98%)
  local copies, waits for them, and re-layouts  0.71 us (2%)
    pallas_call x1, Pallas kernels, shards(): pl.pallas_call(functools.partial(kernel, n), out_shape=pltpu.VMEM((1,) +...  41.4 us

profile of v4, /device:TPU:27, one launch (start us, length us, event | category | flops | bytes accessed | tf_op | source)
XLA Modules:
  0.0 42.1 jit_solution(13412875088849431880)
XLA Ops:
  0.0 41.4 %shard_map.28 = f32[1,2,2,128,128]{4,3,2,1,0:T(8,128)S(1)} custom-call(f32[2,2,128,128]{3,2,1,0:T(8,128)} %init_ref.1, f32[2,128,128]{2,1,0:T(8,128)} %kap_ref.1), custom_call_target="tpu_custom_call" | custom-call | tf_op jit(solution)/shard_map/pallas_call | solution.py:531
  41.4 0.7 %copy.4 = f32[1,2,2,128,128]{4,3,2,1,0:T(8,128)} copy(f32[1,2,2,128,128]{4,3,2,1,0:T(8,128)S(1)} %shard_map.28) | data formatting | bytes 524288

commit v5 on v4

--- a/solution.py
+++ b/solution.py
@@ -303,9 +303,9 @@
 
     def spread(buf, at, cond, t_out=t, t_fin=t, t_fout=t):
         return [
+            copy(buf.at[at], buf.at[0], t_fout, far_out, both(cond, has_out), both(cond, has_far)),
+            copy(buf.at[at], buf.at[4], t_fin, far_in, both(cond, has_far), both(cond, has_out)),
             copy(buf.at[at], buf.at[3], t_out, outer, both(cond, has_out)),
-            copy(buf.at[at], buf.at[4], t_fin, far_in, both(cond, has_far), both(cond, has_out)),
-            copy(buf.at[at], buf.at[0], t_fout, far_out, both(cond, has_out), both(cond, has_far)),
             copy(buf.at[at], buf.at[1], t, partner, cond),
         ]
 
@@ -351,12 +351,16 @@
 
     def correction(i, d):
         even = even_lane()
+        lane = iota(1)
         for j in range(3):
-            for sp, x in enumerate(prolong(d[j])):
+            back, on, back2, on2 = (pltpu.roll(d[j], by, 1) for by in (1, 127, 2, 126))
+            species = (
+                (jnp.where(even, d[j], back), jnp.where(even, back2, on)),
+                (jnp.where(even, on, d[j]), jnp.where(even, back, on2)),
+            )
+            for sp, (x, beside_x) in enumerate(species):
                 pd[i, j, sp] = x
-                low = jnp.where(iota(1) == 0, 0.0, pltpu.roll(x, 1, 1))
-                high = jnp.where(iota(1) == 127, 0.0, pltpu.roll(x, 127, 1))
-                t_ = jnp.where(even, low, high) - 3.0 * x
+                t_ = jnp.where((lane == 0) | (lane == 127), 0.0, beside_x) - 3.0 * x
                 td[i, j, sp, 0] = t_ + row_above(x)
                 td[i, j, sp, 1] = t_ + row_below(x)
 

time: 42.2 us -> 41.5 us (0.983)
  Pallas kernels: 41.4 us -> 40.7 us
    pallas_call x1, Pallas kernels: 41.4 us -> 40.7 us  [shards(): pl.pallas_call(functools.partial(kernel, n), out_shape=pltpu.VMEM((1,) +...]
where the time goes in v5:
time: 41.5 us; the launch traced here: 41.4 us
  Pallas kernels  40.7 us (98%)
  local copies, waits for them, and re-layouts  0.71 us (2%)
    pallas_call x1, Pallas kernels, shards(): pl.pallas_call(functools.partial(kernel, n), out_shape=pltpu.VMEM((1,) +...  40.7 us

profile of v5, /device:TPU:27, one launch (start us, length us, event | category | flops | bytes accessed | tf_op | source)
XLA Modules:
  0.0 41.4 jit_solution(2790068638498470498)
XLA Ops:
  0.0 40.7 %shard_map.28 = f32[1,2,2,128,128]{4,3,2,1,0:T(8,128)S(1)} custom-call(f32[2,2,128,128]{3,2,1,0:T(8,128)} %init_ref.1, f32[2,128,128]{2,1,0:T(8,128)} %kap_ref.1), custom_call_target="tpu_custom_call" | custom-call | tf_op jit(solution)/shard_map/pallas_call | solution.py:535
  40.7 0.7 %copy.4 = f32[1,2,2,128,128]{4,3,2,1,0:T(8,128)} copy(f32[1,2,2,128,128]{4,3,2,1,0:T(8,128)S(1)} %shard_map.28) | data formatting | bytes 524288

commit v6 on v5

--- a/solution.py
+++ b/solution.py
@@ -120,11 +120,20 @@
     has_far = jnp.logical_and(far_in >= 0, far_in < n)
     always = None
     first, second = t == 0, t == 1
-    def other_tm(other):
-        row = jnp.logical_and(other // 2 != me // 2, other // 4 == me // 4)
-        return jnp.where(row, 1 - t, t)
-
-    t_out, t_fin, t_fout = other_tm(outer), other_tm(far_in), other_tm(far_out)
+    def other_tm(other, rows, z, y):
+        chip = other // 2 != me // 2
+        row = jnp.logical_and(chip, other // 4 == me // 4)
+        step_y = other // 16 != me // 16
+        step_z = jnp.logical_and(other // 4 != me // 4, jnp.logical_not(step_y))
+        turn = (other // 2) % 2 != (me // 2) % 2
+        swap = jnp.zeros((), jnp.bool_)
+        for wanted, there in ((rows, row), (z, jnp.logical_and(step_z, turn)), (y, step_y)):
+            if wanted:
+                swap = jnp.logical_or(swap, there)
+        return jnp.where(swap, 1 - t, t)
+
+    t_out, t_fin, t_fout = (other_tm(s, True, False, False) for s in (outer, far_in, far_out))
+    t_inputs, t_late = other_tm(outer, True, True, False), other_tm(outer, True, False, True)
 
     m_out = jnp.where(has_out, 1.0, 0.0).astype(F32)
 
@@ -200,10 +209,10 @@
     for cp in locals_:
         cp.wait()
     p_init = copy(nat.at[1], nat.at[0], t, partner, always)
-    o_init = copy(nat.at[2], nat.at[3], t_out, outer, has_out)
+    o_init = copy(nat.at[2], nat.at[3], t_inputs, outer, has_out)
     p_kap = copy(kn.at[1], kn.at[0], t, partner, always)
-    o_kap = copy(kn.at[2], kn.at[3], t_out, outer, has_out)
-    o_init2 = copy(nat.at[1], nat.at[4], t_out, outer, has_out)
+    o_kap = copy(kn.at[2], kn.at[3], t_inputs, outer, has_out)
+    o_init2 = copy(nat.at[1], nat.at[4], t_inputs, outer, has_out)
     start(p_init, o_init, o_kap, o_init2, p_kap)
 
     def convert(p):
@@ -215,7 +224,7 @@
     ks = sum(kappas(kn, 1) + kappas(kn, 2))
     kc[1] = (0.125 * HALF / 4.0) * pairs(ks, 0.5 * ks)
     p_kc = copy(kc.at[1], kc.at[0], t, partner, always)
-    o_kc = copy(kc.at[1], kc.at[2], t_out, outer, has_out)
+    o_kc = copy(kc.at[1], kc.at[2], t_late, outer, has_out)
 
     def masked(p):
         return jnp.where(p == 3, m_out, 1.0).astype(F32)
@@ -229,7 +238,7 @@
     p_v1 = copy(x1.at[1], x1.at[0], t, partner, always)
     o_v1 = copy(x1.at[1], x1.at[4], t_out, outer, has_out)
     p_v2 = copy(x2.at[1], x2.at[0], t, partner, always)
-    o_v2 = copy(x2.at[1], x2.at[4], t_out, outer, has_out)
+    o_v2 = copy(x2.at[1], x2.at[4], t_late, outer, has_out)
 
     arrived(p_init)
     convert(0)
@@ -432,7 +441,7 @@
         correction(1, [corrected(d11c, b11c, j) - w2s[j] for j in range(3)])
 
     p_v2p = copy(v2p.at[1], v2p.at[0], t, partner, always)
-    r_e = [copy(e3.at[2], e3.at[1], t, outer, has_out), copy(e3.at[2], e3.at[0], t, far_out, has_out, has_far)]
+    r_e = [copy(e3.at[2], e3.at[0], t, far_out, has_out, has_far), copy(e3.at[2], e3.at[1], t, outer, has_out)]
 
     def second_node(p):
         g = fine_rate(v1p, kn, p)

time: 41.5 us -> 40.6 us (0.978)
  Pallas kernels: 40.7 us -> 39.8 us
    pallas_call x1, Pallas kernels: 40.7 us -> 39.8 us  [shards(): pl.pallas_call(functools.partial(kernel, n), out_shape=pltpu.VMEM((1,) +...]
where the time goes in v6:
time: 40.6 us; the launch traced here: 40.5 us
  Pallas kernels  39.8 us (98%)
  local copies, waits for them, and re-layouts  0.71 us (2%)
    pallas_call x1, Pallas kernels, shards(): pl.pallas_call(functools.partial(kernel, n), out_shape=pltpu.VMEM((1,) +...  39.8 us

profile of v6, /device:TPU:27, one launch (start us, length us, event | category | flops | bytes accessed | tf_op | source)
XLA Modules:
  0.0 40.5 jit_solution(6608052578892964438)
XLA Ops:
  0.0 39.8 %shard_map.28 = f32[1,2,2,128,128]{4,3,2,1,0:T(8,128)S(1)} custom-call(f32[2,2,128,128]{3,2,1,0:T(8,128)} %init_ref.1, f32[2,128,128]{2,1,0:T(8,128)} %kap_ref.1), custom_call_target="tpu_custom_call" | custom-call | tf_op jit(solution)/shard_map/pallas_call | solution.py:544
  39.8 0.7 %copy.4 = f32[1,2,2,128,128]{4,3,2,1,0:T(8,128)} copy(f32[1,2,2,128,128]{4,3,2,1,0:T(8,128)S(1)} %shard_map.28) | data formatting | bytes 524288

commit v7 on v6

--- a/solution.py
+++ b/solution.py
@@ -166,6 +166,12 @@
         for _, back, cp in cs:
             when(back, cp.wait_recv)
 
+    barrier = pltpu.get_barrier_semaphore()
+    around = [(has_out, far_out), (has_far, far_in), (has_out, outer), (always, partner)]
+    greet = [(t, cond, s) for cond, s in around] + [(1 - t, cond, s) for cond, s in [(always, me)] + around]
+    for tm, cond, s in greet:
+        when(cond, lambda tm=tm, s=s: pl.semaphore_signal(barrier, inc=1, device_id=(tm, s), device_id_type=MESH))
+
     locals_ = [
         pltpu.make_async_copy(init_ref.at[:, 1 - c], nat.at[1], lsem.at[0]),
         pltpu.make_async_copy(init_ref.at[:, c], nat.at[2], lsem.at[1]),
@@ -174,12 +180,6 @@
     ]
     for cp in locals_:
         cp.start()
-
-    barrier = pltpu.get_barrier_semaphore()
-    around = [(always, partner), (has_out, outer), (has_far, far_in), (has_out, far_out)]
-    greet = [(t, cond, s) for cond, s in around] + [(1 - t, cond, s) for cond, s in [(always, me)] + around]
-    for tm, cond, s in greet:
-        when(cond, lambda tm=tm, s=s: pl.semaphore_signal(barrier, inc=1, device_id=(tm, s), device_id_type=MESH))
 
     @pl.when(jnp.logical_not(has_out))
     def _():

time: 40.6 us -> 40.7 us (level)
  no operation moved by 1% of the time
where the time goes in v7:
time: 40.7 us
  Pallas kernels  39.9 us (98%)
  local copies, waits for them, and re-layouts  0.71 us (2%)
    pallas_call x1, Pallas kernels, shards(): pl.pallas_call(functools.partial(kernel, n), out_shape=pltpu.VMEM((1,) +...  39.9 us

profile of v7, /device:TPU:27, one launch (start us, length us, event | category | flops | bytes accessed | tf_op | source)
XLA Modules:
  0.0 40.7 jit_solution(6043134033701663683)
XLA Ops:
  0.0 39.9 %shard_map.28 = f32[1,2,2,128,128]{4,3,2,1,0:T(8,128)S(1)} custom-call(f32[2,2,128,128]{3,2,1,0:T(8,128)} %init_ref.1, f32[2,128,128]{2,1,0:T(8,128)} %kap_ref.1), custom_call_target="tpu_custom_call" | custom-call | tf_op jit(solution)/shard_map/pallas_call | solution.py:544
  39.9 0.7 %copy.4 = f32[1,2,2,128,128]{4,3,2,1,0:T(8,128)} copy(f32[1,2,2,128,128]{4,3,2,1,0:T(8,128)S(1)} %shard_map.28) | data formatting | bytes 524288
